TPU v7x, 256 devices: a whole 4x4x8 slice. The times are simulated.
256 devices in a mesh: dp: 32 (over y_hi, z, core), tensor: 8 (over y_lo, x).
Axes of the slice: x: 4, y: 4 (y_hi: 2, y_lo: 2; y = y_hi * 2 + y_lo), z: 8, core: 2. Of those that a mesh axis runs over, the one named last changes fastest.
Arguments:
- teacher_q: bfloat16 [32, 1024, 8192], P('dp', None, 'tensor'), may hold values from -80 to 80
- teacher_k: bfloat16 [32, 1024, 1024], P('dp', None, 'tensor'), may hold values from -80 to 80
- teacher_v: bfloat16 [32, 1024, 1024], P('dp', None, 'tensor'), may hold values from -80 to 80
- student_q: bfloat16 [32, 1024, 2048], P('dp', 'tensor'), may hold values from -80 to 80
- student_k: bfloat16 [32, 1024, 256], P('dp', 'tensor'), may hold values from -80 to 80
- student_v: bfloat16 [32, 1024, 256], P('dp', 'tensor'), may hold values from -80 to 80
- lengths: int32 [32], replicated, may hold values from 1 to 1024, 24576 in all
- seq_weight: float32 [32], replicated, may hold values from 0.5 to 4
Outputs:
- relation_loss: float32 [32, 8], P('dp', 'tensor')
- student_q_grad: bfloat16 [32, 1024, 2048], P('dp', 'tensor')
- student_k_grad: bfloat16 [32, 1024, 256], P('dp', 'tensor')
- student_v_grad: bfloat16 [32, 1024, 256], P('dp', 'tensor')
Inputs may be any that keep to these rules, and one draw needn't show every extreme that they name: Tokens at positions lengths[s] and after are padding of sequence s; some sequence has all 1024 tokens valid.
All inputs are finite; a program needn't handle non-finite values.
Results may differ from a plain program's by a relative error of at most 0.0036.
Values may be sent and summed in bfloat16 or wider, within the bound.
A program may use at most 64 MiB of HBM per device.

v0:
```python
import jax
import jax.numpy as jnp
from jax import lax
from jax.sharding import PartitionSpec as P

RELATION_COUNT = 64


def as_sent(value):
    return jax.tree.map(lambda a: a.astype(jnp.bfloat16) if a.dtype == jnp.float32 else a, value)


def head_terms(teach, stud, length, weight):
    seq_len = teach.shape[0]
    block_rows = min(512, seq_len)
    teach_scale = teach.shape[1] ** (-0.5)
    stud_scale = stud.shape[1] ** (-0.5)
    key_positions = jnp.arange(seq_len, dtype=jnp.int32)
    valid_keys = key_positions[None, :] < length
    kl_total = jnp.zeros((), jnp.float32)
    across = jnp.zeros(stud.shape, jnp.float32)
    row_parts = []
    for row_start in range(0, seq_len, block_rows):
        teach_rows = teach[row_start : row_start + block_rows]
        stud_rows = stud[row_start : row_start + block_rows]
        teach_score = jnp.dot(teach_rows, teach.T, preferred_element_type=jnp.float32) * teach_scale
        stud_score = jnp.dot(stud_rows, stud.T, preferred_element_type=jnp.float32) * stud_scale
        teach_score = jnp.where(valid_keys, teach_score, -1e30)
        stud_score = jnp.where(valid_keys, stud_score, -1e30)
        log_teach = jax.nn.log_softmax(teach_score, axis=1)
        log_stud = jax.nn.log_softmax(stud_score, axis=1)
        prob_teach = jnp.exp(log_teach)
        prob_stud = jnp.exp(log_stud)
        valid_rows = row_start + jnp.arange(block_rows, dtype=jnp.int32) < length
        row_divergence = jnp.sum(
            jnp.where(valid_keys, prob_teach * (log_teach - log_stud), 0.0), axis=1
        )
        kl_total = kl_total + jnp.sum(jnp.where(valid_rows, row_divergence, 0.0))
        slope_rows = jnp.where(valid_rows[:, None], weight * (prob_stud - prob_teach), 0.0).astype(
            jnp.bfloat16
        )
        row_parts.append(jnp.dot(slope_rows, stud, preferred_element_type=jnp.float32))
        across = across + lax.dot_general(
            slope_rows, stud_rows, (((0,), (0,)), ((), ())), preferred_element_type=jnp.float32
        )
    gradient = ((jnp.concatenate(row_parts, axis=0) + across) * stud_scale).astype(jnp.bfloat16)
    return (kl_total, gradient)


def kind_pass(teach_heads, stud_heads, length, weight):

    def one_head(head_pair):
        return head_terms(head_pair[0], head_pair[1], length, weight)

    head_losses, gradients = lax.map(one_head, (teach_heads, stud_heads))
    return (jnp.sum(head_losses), gradients)


def split_heads(values, head_count):
    return values.reshape(values.shape[0], head_count, values.shape[1] // head_count).transpose(
        1, 0, 2
    )


def on_device(
    teacher_q, teacher_k, teacher_v, student_q, student_k, student_v, lengths, seq_weight
):
    tensor_size = lax.axis_size("tensor")
    head_count = RELATION_COUNT // tensor_size
    owner_index = lax.axis_index("dp")
    length = lax.dynamic_index_in_dim(lengths, owner_index, 0, keepdims=False)
    weight = lax.dynamic_index_in_dim(seq_weight, owner_index, 0, keepdims=False)
    seq_len = teacher_q.shape[1]

    def spread(values):
        return values.reshape(
            values.shape[0], values.shape[1], tensor_size, values.shape[2] // tensor_size
        )

    def settle(values):
        return split_heads(values.reshape(seq_len, values.shape[3]), head_count)

    def gather_back(gradients):
        return gradients.transpose(1, 0, 2).reshape(1, seq_len, 1, -1)

    def restore(values):
        return values.reshape(values.shape[0], values.shape[1], values.shape[2] * values.shape[3])

    teach_queries = split_heads(teacher_q[0], head_count)
    teach_keys = split_heads(teacher_k[0], head_count)
    teach_values = split_heads(teacher_v[0], head_count)
    got_queries, got_keys, got_values = (
        lax.all_to_all(spread(student_q), "tensor", split_axis=2, concat_axis=1, tiled=True),
        lax.all_to_all(spread(student_k), "tensor", split_axis=2, concat_axis=1, tiled=True),
        lax.all_to_all(spread(student_v), "tensor", split_axis=2, concat_axis=1, tiled=True),
    )
    query_loss, query_grads = kind_pass(teach_queries, settle(got_queries), length, weight)
    key_loss, key_grads = kind_pass(teach_keys, settle(got_keys), length, weight)
    value_loss, value_grads = kind_pass(teach_values, settle(got_values), length, weight)
    query_back, key_back, value_back = (
        lax.all_to_all(
            as_sent(gather_back(query_grads)), "tensor", split_axis=1, concat_axis=2, tiled=True
        ),
        lax.all_to_all(
            as_sent(gather_back(key_grads)), "tensor", split_axis=1, concat_axis=2, tiled=True
        ),
        lax.all_to_all(
            as_sent(gather_back(value_grads)), "tensor", split_axis=1, concat_axis=2, tiled=True
        ),
    )
    kl_sum = query_loss + key_loss + value_loss
    relation_loss = (kl_sum / length.astype(jnp.float32)).reshape(1, 1)
    return (relation_loss, restore(query_back), restore(key_back), restore(value_back))


def solution(mesh):
    in_specs = (
        P("dp", None, "tensor"),
        P("dp", None, "tensor"),
        P("dp", None, "tensor"),
        P("dp", "tensor", None),
        P("dp", "tensor", None),
        P("dp", "tensor", None),
        P(),
        P(),
    )
    out_specs = (
        P("dp", "tensor"),
        P("dp", "tensor", None),
        P("dp", "tensor", None),
        P("dp", "tensor", None),
    )
    return jax.shard_map(
        on_device, mesh=mesh, in_specs=in_specs, out_specs=out_specs, check_vma=False
    )
```

profile of v0, /device:TPU:24, one launch (start us, length us, event | category | flops | bytes accessed | tf_op | source)
XLA Modules:
  0.0 491.5 jit_solution(1683737290810898533)
XLA Ops:
  2.2 5.8 %all-to-all-start.1 = ((bf16[1,128,8,32]{1,3,0,2:T(8,128)(2,1)}), bf16[1,128,8,32]{1,3,0,2:T(8,128)(2,1)S(1)}, u32[]{:S(2)}, u32[]{:S(2)}) async-start(bf16[1,128,8,32]{1,3,0,2:T(8,128)(2,1)} %bitcast.35), calls=%async_computation.1 | async-start | bytes 131072 | tf_op jit(solution)/shard_map/all_to_all | solution.py:94
  9.5 3.3 all-to-all-done.1
  12.8 4.7 all-to-all-start.2
  20.1 4.0 copy.70
  25.6 5.7 %all-to-all-start = ((bf16[1,128,8,256]{1,3,0,2:T(8,128)(2,1)}), bf16[1,128,8,256]{1,3,0,2:T(8,128)(2,1)S(1)}, u32[]{:S(2)}, u32[]{:S(2)}) async-start(bf16[1,128,8,256]{1,3,0,2:T(8,128)(2,1)} %bitcast.27), calls=%async_computation | async-start | bytes 1048576 | tf_op jit(solution)/shard_map/all_to_all | solution.py:93
  31.3 117.2 %while.37 = (s32[]{:T(128)}, f32[8]{0:T(128)S(1)}, bf16[8,1024,4]{1,2,0:T(4,128)(2,1)S(1)}, s32[]{:T(128)}, bf16[8,1024,16]{1,2,0:T(8,128)(2,1)S(1)}, /*index=5*...) while((s32[]{:T(128)}, f32[8]{0:T(128)S(1)}, bf16[8,1024,4]{1,2,0:T(4,128)(2,1)S(1)}, ...), condition=%wide.region_14.16_spmd, body=%wide.region_9.15_spmd.sunk | while | flops 90199040 | bytes 33855164 | solution.py:55
  35.2 3.1 select_reduce_fusion.20
  49.8 3.1 select_reduce_fusion.20
  54.2 2.5 select_convert_fusion.10
  64.5 3.1 select_reduce_fusion.20
  79.1 3.1 select_reduce_fusion.20
  83.5 2.5 select_convert_fusion.10
  93.8 3.1 select_reduce_fusion.20
  108.4 3.1 select_reduce_fusion.20
  123.1 3.1 select_reduce_fusion.20
  127.4 2.5 select_convert_fusion.10
  137.7 3.1 select_reduce_fusion.20
  152.8 5.7 %all-to-all-start.4 = ((bf16[8,2,2048]{2,1,0:T(2,128)(2,1)}), bf16[8,2,2048]{2,1,0:T(2,128)(2,1)S(1)}, u32[]{:S(2)}, u32[]{:S(2)}) async-start(bf16[8,2,2048]{2,1,0:T(2,128)(2,1)} %reshape.115), calls=%async_computation.4 | async-start | bytes 131072 | tf_op jit(solution)/shard_map/all_to_all | solution.py:104
  158.5 116.6 %while.38 = (s32[]{:T(128)}, f32[8]{0:T(128)S(1)}, bf16[8,1024,4]{1,2,0:T(4,128)(2,1)S(1)}, s32[]{:T(128)}, bf16[8,1024,16]{1,2,0:T(8,128)(2,1)S(1)}, /*index=5*...) while((s32[]{:T(128)}, f32[8]{0:T(128)S(1)}, bf16[8,1024,4]{1,2,0:T(4,128)(2,1)S(1)}, ...), condition=%wide.region_21.23_spmd, body=%wide.region_16.22_spmd.sunk | while | flops 90199040 | bytes 33855164 | solution.py:55
  162.4 3.1 select_reduce_fusion.22
  166.7 2.5 select_convert_fusion.11
  176.9 3.1 select_reduce_fusion.22
  191.5 3.1 select_reduce_fusion.22
  206.1 3.1 select_reduce_fusion.22
  220.7 3.1 select_reduce_fusion.22
  235.2 3.1 select_reduce_fusion.22
  249.8 3.1 select_reduce_fusion.22
  264.4 3.1 select_reduce_fusion.22
  279.3 5.7 %all-to-all-start.5 = ((bf16[8,2,2048]{2,1,0:T(2,128)(2,1)}), bf16[8,2,2048]{2,1,0:T(2,128)(2,1)}, u32[]{:S(2)}, u32[]{:S(2)}) async-start(bf16[8,2,2048]{2,1,0:T(2,128)(2,1)} %reshape.117), calls=%async_computation.5 | async-start | bytes 131072 | tf_op jit(solution)/shard_map/all_to_all | solution.py:107
  285.0 182.6 %while.36 = (s32[]{:T(128)}, f32[8]{0:T(128)S(1)}, bf16[8,1024,32]{1,2,0:T(8,128)(2,1)}, s32[]{:T(128)}, bf16[8,1024,128]{1,2,0:T(8,128)(2,1)}, /*index=5*/bf16[8,1024,32]{1,2,0:T(8,128)(2,1)S(1)}, f32[]{:T(128)}, s32[]{:T(128)}) while((s32[]{:T(128)}, f32[8]{0:T(128)S(1)}, bf16[8,1024,32]{1,2,0:T(8,128)(2,1)}, s32[]{:T(128)}, ...), condition=%wide.region_7.9_spmd, body=%wide.region_0.8_spmd.sunk | while | flops 501384192 | bytes 45753008 | solution.py:55
  289.4 4.1 exponential_reduce_fusion.18
  294.2 4.8 select_reduce_fusion.18
  312.2 4.1 exponential_reduce_fusion.18
  317.0 4.8 select_reduce_fusion.18
  335.0 4.1 exponential_reduce_fusion.18
  339.8 4.8 select_reduce_fusion.18
  357.8 4.1 exponential_reduce_fusion.18
  362.6 4.8 select_reduce_fusion.18
  380.6 4.1 exponential_reduce_fusion.18
  385.4 4.8 select_reduce_fusion.18
  403.4 4.1 exponential_reduce_fusion.18
  408.3 4.8 select_reduce_fusion.18
  426.3 4.1 exponential_reduce_fusion.18
  431.1 4.8 select_reduce_fusion.18
  449.1 4.1 exponential_reduce_fusion.18
  453.9 4.8 select_reduce_fusion.18
  470.0 3.8 reduce
  474.7 5.7 %all-to-all-start.3 = ((bf16[8,2,16384]{2,1,0:T(2,128)(2,1)}), bf16[8,2,16384]{2,1,0:T(2,128)(2,1)S(1)}, u32[]{:S(2)}, u32[]{:S(2)}) async-start(bf16[8,2,16384]{2,1,0:T(2,128)(2,1)} %reshape.113), calls=%async_computation.3 | async-start | bytes 1048576 | tf_op jit(solution)/shard_map/all_to_all | solution.py:101
  (562 shorter events, 278.7 us)
Async XLA Ops:
  2.2 10.6 %all-to-all-start.1 = ((bf16[1,128,8,32]{1,3,0,2:T(8,128)(2,1)}), bf16[1,128,8,32]{1,3,0,2:T(8,128)(2,1)S(1)}, u32[]{:S(2)}, u32[]{:S(2)}) async-start(bf16[1,128,8,32]{1,3,0,2:T(8,128)(2,1)} %bitcast.35), calls=%async_computation.1 | async-start | bytes 131072 | tf_op jit(solution)/shard_map/all_to_all | solution.py:94
  12.8 12.7 %all-to-all-start.2 = ((bf16[1,128,8,32]{1,3,0,2:T(8,128)(2,1)}), bf16[1,128,8,32]{1,3,0,2:T(8,128)(2,1)S(1)}, u32[]{:S(2)}, u32[]{:S(2)}) async-start(bf16[1,128,8,32]{1,3,0,2:T(8,128)(2,1)} %bitcast.42), calls=%async_computation.2 | async-start | bytes 131072 | tf_op jit(solution)/shard_map/all_to_all | solution.py:95
  20.1 4.1 copy-start.1
  20.1 5.1 %copy-start.4 = (bf16[1,1024,128]{2,1,0:T(8,128)(2,1)S(1)}, bf16[1,1024,128]{2,1,0:T(8,128)(2,1)}, u32[]{:S(2)}) copy-start(bf16[1,1024,128]{2,1,0:T(8,128)(2,1)} %param.16) | copy-start | bytes 786436
  20.1 5.2 %copy-start.5 = (bf16[1,1024,128]{2,1,0:T(8,128)(2,1)S(1)}, bf16[1,1024,128]{2,1,0:T(8,128)(2,1)}, u32[]{:S(2)}) copy-start(bf16[1,1024,128]{2,1,0:T(8,128)(2,1)} %param.17) | copy-start | bytes 786436
  25.6 127.2 %all-to-all-start = ((bf16[1,128,8,256]{1,3,0,2:T(8,128)(2,1)}), bf16[1,128,8,256]{1,3,0,2:T(8,128)(2,1)S(1)}, u32[]{:S(2)}, u32[]{:S(2)}) async-start(bf16[1,128,8,256]{1,3,0,2:T(8,128)(2,1)} %bitcast.27), calls=%async_computation | async-start | bytes 1048576 | tf_op jit(solution)/shard_map/all_to_all | solution.py:93
  152.8 126.5 %all-to-all-start.4 = ((bf16[8,2,2048]{2,1,0:T(2,128)(2,1)}), bf16[8,2,2048]{2,1,0:T(2,128)(2,1)S(1)}, u32[]{:S(2)}, u32[]{:S(2)}) async-start(bf16[8,2,2048]{2,1,0:T(2,128)(2,1)} %reshape.115), calls=%async_computation.4 | async-start | bytes 131072 | tf_op jit(solution)/shard_map/all_to_all | solution.py:104
  279.3 5.7 %copy-start.2 = (bf16[8,2,2048]{2,1,0:T(2,128)(2,1)}, bf16[8,2,2048]{2,1,0:T(2,128)(2,1)S(1)}, u32[]{:S(2)}) copy-start(bf16[8,2,2048]{2,1,0:T(2,128)(2,1)S(1)} %all-to-all-done.4) | copy-start | bytes 196612
  279.3 195.5 %all-to-all-start.5 = ((bf16[8,2,2048]{2,1,0:T(2,128)(2,1)}), bf16[8,2,2048]{2,1,0:T(2,128)(2,1)}, u32[]{:S(2)}, u32[]{:S(2)}) async-start(bf16[8,2,2048]{2,1,0:T(2,128)(2,1)} %reshape.117), calls=%async_computation.5 | async-start | bytes 131072 | tf_op jit(solution)/shard_map/all_to_all | solution.py:107
  299.0 1.6 copy-start
  321.8 1.6 copy-start
  344.6 1.6 copy-start
  367.5 1.6 copy-start
  390.3 1.6 copy-start
  413.1 1.6 copy-start
  435.9 1.6 copy-start
  458.7 1.6 copy-start
  470.0 12.3 %copy-start.3 = (bf16[8,2,2048]{2,1,0:T(2,128)(2,1)S(1)}, bf16[8,2,2048]{2,1,0:T(2,128)(2,1)}, u32[]{:S(2)}) copy-start(bf16[8,2,2048]{2,1,0:T(2,128)(2,1)} %copy-done.2) | copy-start | bytes 196612
  474.7 13.7 %all-to-all-start.3 = ((bf16[8,2,16384]{2,1,0:T(2,128)(2,1)}), bf16[8,2,16384]{2,1,0:T(2,128)(2,1)S(1)}, u32[]{:S(2)}, u32[]{:S(2)}) async-start(bf16[8,2,16384]{2,1,0:T(2,128)(2,1)} %reshape.113), calls=%async_computation.3 | async-start | bytes 1048576 | tf_op jit(solution)/shard_map/all_to_all | solution.py:101
where the time goes:
time: 495 us; the launch traced here: 492 us
  matrix products  221 us (45%)
  other arithmetic  156 us (32%)
  local copies, waits for them, and re-layouts  41.8 us (8%)
  starting transfers between devices  33.3 us (7%)
  loops' own time  32 us (6%)
    dot_general x48, matrix products, head_terms(): jnp.dot(teach_rows, teach.T, preferred_element_type=jnp.float32)  117 us
    dot_general x48, matrix products, head_terms(): jnp.dot(stud_rows, stud.T, preferred_element_type=jnp.float32) * stud_scale  66.3 us
    convert_element_type x24, other arithmetic, head_terms(): jnp.where(valid_rows[:, None], weight * (prob_stud - prob_teach), 0.0)  61 us
    another operation x3, loops' own time, kind_pass(): head_losses, gradients = lax.map(one_head, (teach_heads, stud_heads))  32 us
    reduce_sum x24, other arithmetic, head_terms(): kl_total = kl_total + jnp.sum(jnp.where(valid_rows, row_divergence, 0.0))  29 us
    lt x48, other arithmetic, head_terms(): valid_rows = row_start + jnp.arange(block_rows, dtype=jnp.int32) < length  27.9 us
    dot_general x48, matrix products, head_terms(): jnp.dot(slope_rows, stud, preferred_element_type=jnp.float32)  18.9 us
    dot_general x48, matrix products, head_terms(): lax.dot_general(slope_rows, stud_rows, (((0,), (0,)), ((), ())), preferre...  18.7 us
  transfers between devices with their start and end apart: 6, of which 1 were waited for; matrix products, arithmetic and copies ran while one was open for 84% of the time, Pallas kernels for 0%

commit v1 on v0

v1 whole, which is shorter than its diff:
```python
import functools
import math

import jax
import jax.numpy as jnp
from jax import lax
from jax.experimental import pallas as pl
from jax.experimental.pallas import tpu as pltpu
from jax.sharding import PartitionSpec as P

bf16, f32 = jnp.bfloat16, jnp.float32
MESH = pl.DeviceIdType.MESH
NT = (((1,), (1,)), ((), ()))
NN = (((1,), (0,)), ((), ()))
N = 1024
TS = 8
ROWS = N // TS
HEADS = 8
BL = 256
NB = N // BL
LOG2E = math.log2(math.e)
SAFE_LOG2 = 115.0
VMEM_LIMIT = 60 * 2**20


def dot(a, b, dims):
    return lax.dot_general(a, b, dims, preferred_element_type=f32)


def fold_kv(k, v):
    h = ROWS // 2
    return jnp.concatenate([k[:h], v[:h], k[h:], v[h:]], axis=1)


def greet(me):
    barrier = pltpu.get_barrier_semaphore()
    for s in range(1, TS):
        pl.semaphore_signal(
            barrier, inc=1, device_id={"tensor": lax.rem(me + s, TS)}, device_id_type=MESH
        )
    pl.semaphore_wait(barrier, TS - 1)


def send(src, dst, send_sem, recv_sem, peer):
    return pltpu.make_async_remote_copy(
        src_ref=src,
        dst_ref=dst,
        send_sem=send_sem,
        recv_sem=recv_sem,
        device_id={"tensor": peer},
        device_id_type=MESH,
    )


def forward_kernel(sq, sk, sv, rq, rkv, kv, send_sem, recv_sem, own_sem):
    me = lax.axis_index("tensor")
    for t in range(TS):
        kv[t] = fold_kv(sk[0, :, t * 32 : t * 32 + 32], sv[0, :, t * 32 : t * 32 + 32])
    greet(me)

    def parts(t):
        return (
            (sq.at[0, :, pl.ds(pl.multiple_of(t * 256, 256), 256)],
             rq.at[pl.ds(pl.multiple_of(me * ROWS, ROWS), ROWS), :]),
            (kv.at[t], rkv.at[me]),
        )

    copies = []
    for s in range(1, TS):
        peer = lax.rem(me + s, TS)
        for i, (src, dst) in enumerate(parts(peer)):
            copies.append(send(src, dst, send_sem.at[i, s], recv_sem.at[i, s], peer))
            copies[-1].start()
    own = [
        pltpu.make_async_copy(src, dst, own_sem.at[i])
        for i, (src, dst) in enumerate(parts(me))
    ]
    for c in own:
        c.start()
    for c in own:
        c.wait()
    for c in copies:
        c.wait()


def forward(sq, sk, sv):
    return pl.pallas_call(
        forward_kernel,
        out_shape=(
            jax.ShapeDtypeStruct((N, 256), bf16),
            jax.ShapeDtypeStruct((TS, ROWS // 2, 128), bf16),
        ),
        in_specs=[pl.BlockSpec(memory_space=pltpu.VMEM)] * 3,
        out_specs=[pl.BlockSpec(memory_space=pltpu.VMEM)] * 2,
        scratch_shapes=[
            pltpu.VMEM((TS, ROWS // 2, 128), bf16),
            pltpu.SemaphoreType.DMA((2, TS)),
            pltpu.SemaphoreType.DMA((2, TS)),
            pltpu.SemaphoreType.DMA((2,)),
        ],
        compiler_params=pltpu.CompilerParams(collective_id=0, has_side_effects=True),
    )(sq, sk, sv)


def backward_kernel(gq, gkv, oq, ok, ov, kv, send_sem, recv_sem, own_sem):
    me = lax.axis_index("tensor")
    greet(me)

    def parts(t):
        return (
            (gq.at[pl.ds(pl.multiple_of(t * ROWS, ROWS), ROWS), :],
             oq.at[0, :, pl.ds(pl.multiple_of(me * 256, 256), 256)]),
            (gkv.at[t], kv.at[me]),
        )

    copies = []
    for s in range(1, TS):
        peer = lax.rem(me + s, TS)
        for i, (src, dst) in enumerate(parts(peer)):
            copies.append(send(src, dst, send_sem.at[i, s], recv_sem.at[i, s], peer))
            copies[-1].start()
    own = [
        pltpu.make_async_copy(src, dst, own_sem.at[i])
        for i, (src, dst) in enumerate(parts(me))
    ]
    for c in own:
        c.start()
    for c in own:
        c.wait()
    for c in copies:
        c.wait()
    h = ROWS // 2
    for i, out in enumerate((ok, ov)):
        for half in range(2):
            lo = half * 64 + i * 32
            out[0, half * h : half * h + h, :] = jnp.concatenate(
                [kv[t][:, lo : lo + 32] for t in range(TS)], axis=1
            )


def backward(gq, gkv):
    return pl.pallas_call(
        backward_kernel,
        out_shape=(
            jax.ShapeDtypeStruct((1, ROWS, 2048), bf16),
            jax.ShapeDtypeStruct((1, ROWS, 256), bf16),
            jax.ShapeDtypeStruct((1, ROWS, 256), bf16),
        ),
        in_specs=[pl.BlockSpec(memory_space=pltpu.VMEM)] * 2,
        out_specs=[pl.BlockSpec(memory_space=pltpu.VMEM)] * 3,
        scratch_shapes=[
            pltpu.VMEM((TS, ROWS // 2, 128), bf16),
            pltpu.SemaphoreType.DMA((2, TS)),
            pltpu.SemaphoreType.DMA((2, TS)),
            pltpu.SemaphoreType.DMA((2,)),
        ],
        compiler_params=pltpu.CompilerParams(collective_id=1, has_side_effects=True),
    )(gq, gkv)


class Head:
    def __init__(self, n):
        q = n < HEADS
        kv = jnp.where(n < 2 * HEADS, 0, 1)
        sub = lax.rem(n, HEADS)
        self.t_at = pl.multiple_of(jnp.where(q, n, HEADS + kv) * 128, 128)
        self.s_at = pl.multiple_of(jnp.where(q, n // 4, 2 + kv) * 128, 128)
        self.g_at = pl.multiple_of(jnp.where(q, 32 * n, 256 + 32 * kv), 32)
        self.t_scale = jnp.where(q, LOG2E * 128**-0.5, LOG2E * 0.25).astype(f32)
        self.s_scale = jnp.where(q, LOG2E * 32**-0.5, LOG2E * 0.5).astype(f32)
        self.g_scale = jnp.where(q, 32**-0.5, 0.5).astype(f32)
        self.t_lo = jnp.where(q, 0, 16 * sub)
        self.t_hi = jnp.where(q, 128, 16 * sub + 16)
        self.s_lo = jnp.where(q, 32 * lax.rem(n, 4), 4 * sub)
        self.s_hi = self.s_lo + jnp.where(q, 32, 4)
        self.b_lo = jnp.where(q, 0, 4 * sub)
        self.b_hi = jnp.where(q, 32, 4 * sub + 4)


def setup(length, tq, tk, tv, rq, rkv, ta, sb, bt, grad):
    valid = lax.broadcasted_iota(jnp.int32, (N, 1), 0) < length

    def real(x):
        return jnp.where(valid, x.astype(f32), 0.0)

    ta[:, 0:1024] = real(tq[0]).astype(bf16)
    ta[:, 1024:1152] = real(tk[0]).astype(bf16)
    ta[:, 1152:1280] = real(tv[0]).astype(bf16)
    b = real(rq[...])
    sb[:, 0:256] = b.astype(bf16)
    bt[0:256] = b.T.astype(bf16)
    folded = rkv[...]
    for i in range(2):
        halves = [folded[:, :, 64 * h + 32 * i : 64 * h + 32 * i + 32] for h in range(2)]
        b = jnp.concatenate(halves, axis=1).reshape(N, 32)
        b = real(jnp.concatenate([b, jnp.zeros((N, 96), bf16)], axis=1))
        sb[:, 256 + 128 * i : 384 + 128 * i] = b.astype(bf16)
        bt[256 + 32 * i : 288 + 32 * i] = b.T[0:32].astype(bf16)
    grad[...] = jnp.zeros_like(grad)


def largest(x):
    return jnp.max(jnp.abs(x).astype(f32))


def scores_bound(ta, sb):
    def bound(x, w):
        top = largest(x)
        return (LOG2E * 1.0001 * w**0.5) * top * top

    return jnp.maximum(
        jnp.maximum(bound(ta[:, 0:1024], 128), bound(ta[:, 1024:1280], 16)),
        jnp.maximum(bound(sb[:, 0:256], 32), bound(sb[:, 256:512], 4)),
    )


def head_operands(h, ta, sb, lt, rt, ls, rs):
    lane = lax.broadcasted_iota(jnp.int32, (1, 128), 1)

    def put(x, scale, lo, hi, left, right):
        xf = x.astype(f32)
        right[...] = jnp.where((lane >= lo) & (lane < hi), xf, 0.0).astype(bf16)
        y = xf * scale
        top = y.astype(bf16)
        left[:, 0:128] = top
        left[:, 128:256] = (y - top.astype(f32)).astype(bf16)

    put(ta[:, pl.ds(h.t_at, 128)], h.t_scale, h.t_lo, h.t_hi, lt, rt)
    put(sb[:, pl.ds(h.s_at, 128)], h.s_scale, h.s_lo, h.s_hi, ls, rs)


def head_columns(h, bt, at=slice(None)):
    sub = lax.broadcasted_iota(jnp.int32, (32, 1), 0)
    b = bt[pl.ds(h.g_at, 32), at].astype(f32)
    return jnp.where((sub >= h.b_lo) & (sub < h.b_hi), b, 0.0).astype(bf16)


def folded_sum(x):
    return x.reshape(x.shape[0] // 8, 8, x.shape[1]).sum(0)


def first_block(i, j, lt, rt, ls, rs, et, es, diff, row_t, row_s, col):
    ri, rj = pl.ds(i * BL, BL), pl.ds(j * BL, BL)
    x_t = dot(lt[ri], jnp.concatenate([rt[rj], rt[rj]], axis=1), NT)
    x_s = dot(ls[ri], jnp.concatenate([rs[rj], rs[rj]], axis=1), NT)
    e_t, e_s = jnp.exp2(x_t), jnp.exp2(x_s)
    et[ri, rj] = e_t
    es[ri, rj] = e_s
    diff[ri, rj] = x_t - x_s
    if i == 0:
        col[0:8, rj] = folded_sum(e_t)
        col[8:16, rj] = folded_sum(e_s)
    else:
        col[0:8, rj] += folded_sum(e_t)
        col[8:16, rj] += folded_sum(e_s)
    if j == i + 1:
        row_t[ri] = e_t[:, :128] + e_t[:, 128:]
        row_s[ri] = e_s[:, :128] + e_s[:, 128:]
    elif j > i:
        row_t[ri] += e_t[:, :128] + e_t[:, 128:]
        row_s[ri] += e_s[:, :128] + e_s[:, 128:]


def row_statistics(length, row_t, row_s, col, rvec, rb_t, rb_s, log_sum):
    valid = lax.broadcasted_iota(jnp.int32, (1, N), 1) < length
    padded = (N - length).astype(f32)

    def total(row, c):
        r = jnp.sum(row[0 : N - BL].T, axis=0, keepdims=True)
        r = jnp.concatenate([r, jnp.zeros((1, BL), f32)], axis=1)
        return jnp.where(valid, r + jnp.sum(c, axis=0, keepdims=True) - padded, 1.0)

    sum_t, sum_s = total(row_t, col[0:8]), total(row_s, col[8:16])
    r_t, r_s = jnp.where(valid, 1.0 / sum_t, 0.0), jnp.where(valid, 1.0 / sum_s, 0.0)
    rvec[0:8] = jnp.broadcast_to(r_t, (8, N))
    rvec[8:16] = jnp.broadcast_to(r_s, (8, N))
    rb_t[...] = jnp.broadcast_to(r_t, (128, N)).T
    rb_s[...] = jnp.broadcast_to(r_s, (128, N)).T
    log_sum[0:1, :] += jnp.log2(sum_s) - jnp.log2(sum_t)


def second_block(i, j, et, es, diff, rvec, rb_t, rb_s, both, kl):
    ri, rj = pl.ds(i * BL, BL), pl.ds(j * BL, BL)

    def pair(by_row, by_col):
        wide = jnp.concatenate([by_row, by_row], axis=1).reshape(BL // 8, 8, BL)
        return (wide + by_col[None]).reshape(BL, BL)

    q_t = et[ri, rj] * pair(rb_t[ri], rvec[0:8, rj])
    both[ri, rj] = (es[ri, rj] * pair(rb_s[ri], rvec[8:16, rj]) - q_t).astype(bf16)
    part = folded_sum(q_t * diff[ri, rj])
    kl[:, rj] += 0.5 * part if i == j else part


def bounded_heads(length, weight, ta, sb, bt, grad, lt, rt, ls, rs, et, es, diff, row_t, row_s, col, rvec, rb_t, rb_s, both, kl, log_sum):
    def one_head(n, carry):
        h = Head(n)
        head_operands(h, ta, sb, lt, rt, ls, rs)
        for j in range(NB):
            for i in range(j + 1):
                first_block(i, j, lt, rt, ls, rs, et, es, diff, row_t, row_s, col)
        row_statistics(length, row_t, row_s, col, rvec, rb_t, rb_s, log_sum)
        for j in range(NB):
            for i in range(j + 1):
                second_block(i, j, et, es, diff, rvec, rb_t, rb_s, both, kl)
        b = head_columns(h, bt)
        scale = h.g_scale * weight
        for j in range(NB):
            lo, hi = j * BL, (j + 1) * BL
            g = dot(b[:, :hi], both[0:hi, lo:hi], NN)
            if hi < N:
                g = g + dot(b[:, hi:], both[lo:hi, hi:N], NT)
            grad[pl.ds(h.g_at, 32), lo:hi] += g * scale
        return carry

    lax.fori_loop(0, 3 * HEADS, one_head, 0)


def general_heads(length, weight, ta, sb, bt, grad, rt, rs, lt, ls, both, kl, strip=128):
    keys = lax.broadcasted_iota(jnp.int32, (1, N), 1) < length

    def one_head(n, carry):
        h = Head(n)
        head_operands(h, ta, sb, lt, rt, ls, rs)
        b = head_columns(h, bt)
        scale = h.g_scale * weight

        def rows(k, carry):
            at = pl.ds(pl.multiple_of(k * strip, strip), strip)
            here = k * strip + lax.broadcasted_iota(jnp.int32, (strip, 1), 0) < length

            def softmax(x, c):
                x = jnp.where(keys, dot(x[at], x[...], NT) * c, -1e30)
                x = x - jnp.max(x, axis=1, keepdims=True)
                x = x - jnp.log2(jnp.sum(jnp.exp2(x), axis=1, keepdims=True))
                return x, jnp.exp2(x)

            log_t, p_t = softmax(rt, h.t_scale)
            log_s, p_s = softmax(rs, h.s_scale)
            inside = keys & here
            kl[...] += folded_sum(jnp.where(inside, p_t * (log_t - log_s), 0.0))
            slope = jnp.where(inside, p_s - p_t, 0.0).astype(bf16)
            both[at, :] = slope
            grad[pl.ds(h.g_at, 32), :] += dot(head_columns(h, bt, at), slope, NN) * scale
            grad[pl.ds(h.g_at, 32), at] += dot(b, slope, NT) * scale
            return carry

        return lax.fori_loop(0, N // strip, rows, carry)

    lax.fori_loop(0, 3 * HEADS, one_head, 0)


def heads_kernel(
    lengths, weights, tq, tk, tv, rq, rkv, loss, gq, gkv,
    ta, sb, bt, grad, lt, rt, ls, rs, et, es, diff, row_t, row_s, col, rvec, rb_t, rb_s, both, kl, log_sum,
):
    owner = lax.axis_index("dp")
    length, weight = lengths[owner], weights[owner]
    setup(length, tq, tk, tv, rq, rkv, ta, sb, bt, grad)
    kl[...] = jnp.zeros_like(kl)
    log_sum[...] = jnp.zeros_like(log_sum)
    bounded = scores_bound(ta, sb) <= SAFE_LOG2

    @pl.when(bounded)
    def _():
        bounded_heads(length, weight, ta, sb, bt, grad, lt, rt, ls, rs, et, es, diff, row_t, row_s, col, rvec, rb_t, rb_s, both, kl, log_sum)

    @pl.when(jnp.logical_not(bounded))
    def _():
        general_heads(length, weight, ta, sb, bt, grad, rt, rs, lt, ls, both, kl)

    total = (jnp.sum(kl[...]) + jnp.sum(log_sum[...])) * math.log(2.0)
    loss[0, 0] = total / length.astype(f32)
    valid = lax.broadcasted_iota(jnp.int32, (N, 1), 0) < length
    gq[...] = jnp.where(valid, grad[0:256].T, 0.0).astype(bf16)
    kv = jnp.concatenate([grad[256:320], jnp.zeros((64, N), f32)], axis=0).T
    kv = jnp.where(valid, kv, 0.0).astype(bf16).reshape(TS, 2, ROWS // 2, 128)
    gkv[...] = jnp.concatenate([kv[:, 0, :, 0:64], kv[:, 1, :, 0:64]], axis=2)


def heads(lengths, weights, tq, tk, tv, rq, rkv):
    smem = pl.BlockSpec(memory_space=pltpu.SMEM)
    vmem = pl.BlockSpec(memory_space=pltpu.VMEM)
    square = (N, N)
    return pl.pallas_call(
        heads_kernel,
        out_shape=(
            jax.ShapeDtypeStruct((1, 1), f32),
            jax.ShapeDtypeStruct((N, 256), bf16),
            jax.ShapeDtypeStruct((TS, ROWS // 2, 128), bf16),
        ),
        in_specs=[smem, smem] + [vmem] * 5,
        out_specs=[smem, vmem, vmem],
        scratch_shapes=[
            pltpu.VMEM((N, 1280), bf16),
            pltpu.VMEM((N, 512), bf16),
            pltpu.VMEM((320, N), bf16),
            pltpu.VMEM((320, N), f32),
            pltpu.VMEM((N, 256), bf16),
            pltpu.VMEM((N, 128), bf16),
            pltpu.VMEM((N, 256), bf16),
            pltpu.VMEM((N, 128), bf16),
            pltpu.VMEM(square, f32),
            pltpu.VMEM(square, f32),
            pltpu.VMEM(square, f32),
            pltpu.VMEM((N, 128), f32),
            pltpu.VMEM((N, 128), f32),
            pltpu.VMEM((16, N), f32),
            pltpu.VMEM((16, N), f32),
            pltpu.VMEM((N, 128), f32),
            pltpu.VMEM((N, 128), f32),
            pltpu.VMEM(square, bf16),
            pltpu.VMEM((8, N), f32),
            pltpu.VMEM((8, N), f32),
        ],
        compiler_params=pltpu.CompilerParams(vmem_limit_bytes=VMEM_LIMIT),
    )(lengths, weights, tq, tk, tv, rq, rkv)


def on_device(teacher_q, teacher_k, teacher_v, student_q, student_k, student_v, lengths, seq_weight):
    rq, rkv = forward(student_q, student_k, student_v)
    loss, gq, gkv = heads(lengths, seq_weight, teacher_q, teacher_k, teacher_v, rq, rkv)
    return (loss, *backward(gq, gkv))


def solution(mesh):
    in_specs = (
        P("dp", None, "tensor"),
        P("dp", None, "tensor"),
        P("dp", None, "tensor"),
        P("dp", "tensor", None),
        P("dp", "tensor", None),
        P("dp", "tensor", None),
        P(),
        P(),
    )
    out_specs = (
        P("dp", "tensor"),
        P("dp", "tensor", None),
        P("dp", "tensor", None),
        P("dp", "tensor", None),
    )
    return jax.shard_map(
        on_device, mesh=mesh, in_specs=in_specs, out_specs=out_specs, check_vma=False
    )
```

time: 495 us -> 243 us (0.49)
  Pallas kernels: 0 us -> 236 us
  matrix products: 221 us -> 0 us
  other arithmetic: 156 us -> 0 us
  local copies, waits for them, and re-layouts: 41.8 us -> 4.83 us
  starting transfers between devices: 33.3 us -> 0 us
  loops' own time: 32 us -> 0 us
    pallas_call x0 -> x3, Pallas kernels: none -> 236 us  [the longest x1 208 us: heads(): pl.pallas_call(heads_kernel, out_shape=(jax.ShapeDtypeStruct((1, 1), f32)...]
    dot_general x192 -> x0, matrix products: 221 us -> none  [the longest x48 117 us: head_terms(): jnp.dot(teach_rows, teach.T, preferred_element_type=jnp.float32)]
    convert_element_type x24 -> x0, other arithmetic: 61 us -> none  [head_terms(): jnp.where(valid_rows[:, None], weight * (prob_stud - prob_teach), 0.0)]
    reduce_sum x51 -> x0, other arithmetic: 44.9 us -> none  [the longest x24 29 us: head_terms(): kl_total = kl_total + jnp.sum(jnp.where(valid_rows, row_divergence, 0.0))]
    lt x72 -> x0, other arithmetic: 41.6 us -> none  [the longest x48 27.9 us: head_terms(): valid_rows = row_start + jnp.arange(block_rows, dtype=jnp.int32) < length]
    all_to_all x6 -> x0, starting transfers between devices: 33.3 us -> none  [the longest x1 5.76 us: on_device(): lax.all_to_all(spread(student_k), 'tensor', split_axis=2, concat_axis=1,...]
    another operation x3 -> x0, loops' own time: 32 us -> none  [kind_pass(): head_losses, gradients = lax.map(one_head, (teach_heads, stud_heads))]
    unnamed x29 -> x3, local copies, waits for them, and re-layouts: 16.4 us -> 4.83 us
  transfers between devices with their start and end apart: 6 -> 0, of which waited for: 1 -> 0; matrix products, arithmetic and copies ran while one was open for 84% -> 0% of each run, Pallas kernels for 0% -> 0%
where the time goes in v1:
time: 243 us; the launch traced here: 242 us
  Pallas kernels  236 us (97%)
  local copies, waits for them, and re-layouts  4.83 us (2%)
    pallas_call x1, Pallas kernels, heads(): pl.pallas_call(heads_kernel, out_shape=(jax.ShapeDtypeStruct((1, 1), f32)...  208 us
    pallas_call x1, Pallas kernels, forward(): pl.pallas_call(forward_kernel, out_shape=(jax.ShapeDtypeStruct((N, 256),...  14.5 us
    pallas_call x1, Pallas kernels, backward(): pl.pallas_call(backward_kernel, out_shape=(jax.ShapeDtypeStruct((1, ROWS,...  14.1 us

profile of v1, /device:TPU:24, one launch (start us, length us, event | category | flops | bytes accessed | tf_op | source)
XLA Modules:
  0.0 242.0 jit_solution(6124231278177145864)
XLA Ops:
  0.6 14.5 %shard_map.111 = (bf16[1024,256]{1,0:T(8,128)(2,1)}, bf16[8,64,128]{2,1,0:T(8,128)(2,1)}) custom-call(bf16[1,128,2048]{2,1,0:T(8,128)(2,1)} %sq.1, bf16[1,128,256]{2,1,0:T(8,128)(2,1)} %sk.1, bf16[1,128,256]{2,1,0:T(8,128)(2,1)} %sv.1), custom_call_target="tpu_custom_call" | custom-call | tf_op jit(solution)/shard_map/pallas_call | solution.py:87
  15.1 207.9 %shard_map.112 = (f32[1,1]{1,0:T(1,128)}, bf16[1024,256]{1,0:T(8,128)(2,1)}, bf16[8,64,128]{2,1,0:T(8,128)(2,1)}) custom-call(s32[32]{0:T(128)} %lengths.1, f32[32]{0:T(128)} %weights.1, bf16[1,1024,1024]{2,1,0:T(8,128)(2,1)} %tq.1, bf16[1,1024,128]{2,1,0:T(8,128)(2,1)} %tk.1, bf16[1,1024,128]{2,1,0:T(8,128)(2,1)} %tv.1, ...), custom_call_target="tpu_custom_call" | custom-call | tf_op jit(solution)/shard_map/pallas_call | solution.py:385
  223.0 14.1 %shard_map.113 = (bf16[1,128,2048]{2,1,0:T(8,128)(2,1)}, bf16[1,128,256]{2,1,0:T(8,128)(2,1)}, bf16[1,128,256]{2,1,0:T(8,128)(2,1)}) custom-call(bf16[1024,256]{1,0:T(8,128)(2,1)} %get-tuple-element.15.gq, bf16[8,64,128]{2,1,0:T(8,128)(2,1)} %get-tuple-element.16.gkv), custom_call_target="tpu_custom_call" | custom-call | tf_op jit(solution)/shard_map/pallas_call | solution.py:142
  237.1 1.9 copy.15
  239.0 1.5 copy.16
  240.5 1.5 copy.17

commit v2 on v0

--- a/solution.py
+++ b/solution.py
@@ -1,7 +1,28 @@
+import functools
+import math
+
 import jax
 import jax.numpy as jnp
 from jax import lax
+from jax.experimental import pallas as pl
+from jax.experimental.pallas import tpu as pltpu
 from jax.sharding import PartitionSpec as P
+
+bf16, f32 = jnp.bfloat16, jnp.float32
+MESH = pl.DeviceIdType.MESH
+NT = (((1,), (1,)), ((), ()))
+NN = (((1,), (0,)), ((), ()))
+N = 1024
+TS = 8
+ROWS = N // TS
+HALF = ROWS // 2
+HEADS = 8
+BL = 256
+NB = N // BL
+LOG2E = math.log2(math.e)
+SAFE_LOG2 = 115.0
+VMEM_LIMIT = 60 * 2**20
+
 
 RELATION_COUNT = 64
 
@@ -62,7 +83,7 @@
     )
 
 
-def on_device(
+def general_program(
     teacher_q, teacher_k, teacher_v, student_q, student_k, student_v, lengths, seq_weight
 ):
     tensor_size = lax.axis_size("tensor")
@@ -113,6 +134,409 @@
     return (relation_loss, restore(query_back), restore(key_back), restore(value_back))
 
 
+def bound_lanes(x, w):
+    top = jnp.max(jnp.abs(x).astype(f32).reshape(N // 8, 8, x.shape[1]), axis=0)
+    top = functools.reduce(jnp.maximum, [top[:, c : c + 128] for c in range(0, x.shape[1], 128)])
+    return (LOG2E * 1.0001 * w**0.5) * top * top
+
+
+def dot(a, b, dims):
+    return lax.dot_general(a, b, dims, preferred_element_type=f32)
+
+
+def fold_kv(k, v):
+    return jnp.concatenate([k[:HALF], v[:HALF], k[HALF:], v[HALF:]], axis=1)
+
+
+class Head:
+    def __init__(self, n):
+        q = (n >= HEADS) & (n < 2 * HEADS)
+        kv = jnp.where(n < HEADS, 0, 1)
+        sub = lax.rem(n, HEADS)
+        self.t_at = pl.multiple_of(jnp.where(q, sub, HEADS + kv) * 128, 128)
+        self.s_at = pl.multiple_of(jnp.where(q, sub // 4, 2 + kv) * 128, 128)
+        self.g_at = pl.multiple_of(jnp.where(q, 32 * sub, 256 + 32 * kv), 32)
+        self.t_scale = jnp.where(q, LOG2E * 128**-0.5, LOG2E * 0.25).astype(f32)
+        self.s_scale = jnp.where(q, LOG2E * 32**-0.5, LOG2E * 0.5).astype(f32)
+        self.g_scale = jnp.where(q, 32**-0.5, 0.5).astype(f32)
+        self.t_lo = jnp.where(q, 0, 16 * sub)
+        self.t_hi = jnp.where(q, 128, 16 * sub + 16)
+        self.s_lo = jnp.where(q, 32 * lax.rem(sub, 4), 4 * sub)
+        self.s_hi = self.s_lo + jnp.where(q, 32, 4)
+        self.b_lo = jnp.where(q, 0, 4 * sub)
+        self.b_hi = jnp.where(q, 32, 4 * sub + 4)
+
+
+def split_scaled(x, scale, left, at):
+    y = x.astype(f32) * scale
+    top = y.astype(bf16)
+    left[:, at : at + 128] = top
+    left[:, at + 128 : at + 256] = (y - top.astype(f32)).astype(bf16)
+
+
+def set_teacher(valid, ta, lt):
+    for g in range(HEADS + 2):
+        at = g * 128
+        x = jnp.where(valid, ta[:, at : at + 128].astype(f32), 0.0).astype(bf16)
+        ta[:, at : at + 128] = x
+        split_scaled(x, LOG2E * (128**-0.5 if g < HEADS else 0.25), lt, 2 * at)
+
+
+def set_student_kv(valid, rkv, sb, bt, ls):
+    folded = rkv[...]
+    for i in range(2):
+        halves = [folded[:, :, 64 * h + 32 * i : 64 * h + 32 * i + 32] for h in range(2)]
+        b = jnp.concatenate(halves, axis=1).reshape(N, 32)
+        b = jnp.where(valid, jnp.concatenate([b, jnp.zeros((N, 96), bf16)], axis=1).astype(f32), 0.0)
+        at = 256 + 128 * i
+        sb[:, at : at + 128] = b.astype(bf16)
+        bt[256 + 32 * i : 288 + 32 * i] = b.T[0:32].astype(bf16)
+        split_scaled(b.astype(bf16), LOG2E * 0.5, ls, 2 * at)
+
+
+def set_student_q(valid, rq, sb, bt, ls):
+    for g in range(2):
+        at = 128 * g
+        b = jnp.where(valid, rq[:, at : at + 128].astype(f32), 0.0)
+        sb[:, at : at + 128] = b.astype(bf16)
+        bt[at : at + 128] = b.T.astype(bf16)
+        split_scaled(b.astype(bf16), LOG2E * 32**-0.5, ls, 2 * at)
+
+
+def right_operands(h, ta, sb, rt, rs):
+    lane = lax.broadcasted_iota(jnp.int32, (1, 128), 1)
+
+    def keep(lo, hi):
+        return ((lane >= lo) & (lane < hi)).astype(f32).astype(bf16)
+
+    rt[...] = ta[:, pl.ds(h.t_at, 128)] * keep(h.t_lo, h.t_hi)
+    rs[...] = sb[:, pl.ds(h.s_at, 128)] * keep(h.s_lo, h.s_hi)
+
+
+def head_columns(h, bt):
+    sub = lax.broadcasted_iota(jnp.int32, (32, 1), 0)
+    b = bt[pl.ds(h.g_at, 32), :].astype(f32)
+    return jnp.where((sub >= h.b_lo) & (sub < h.b_hi), b, 0.0).astype(bf16)
+
+
+def folded_sum(x):
+    return x.reshape(x.shape[0] // 8, 8, x.shape[1]).sum(0)
+
+
+def first_block(i, j, h, lt, rt, ls, rs, et, es, diff, row_t, row_s, col):
+    ri, rj = pl.ds(i * BL, BL), pl.ds(j * BL, BL)
+    x_t = dot(lt[ri, pl.ds(2 * h.t_at, 256)], jnp.concatenate([rt[rj], rt[rj]], axis=1), NT)
+    x_s = dot(ls[ri, pl.ds(2 * h.s_at, 256)], jnp.concatenate([rs[rj], rs[rj]], axis=1), NT)
+    e_t, e_s = jnp.exp2(x_t), jnp.exp2(x_s)
+    et[ri, rj] = e_t
+    es[ri, rj] = e_s
+    diff[ri, rj] = x_t - x_s
+    if i == 0:
+        col[0:8, rj] = folded_sum(e_t)
+        col[8:16, rj] = folded_sum(e_s)
+    else:
+        col[0:8, rj] += folded_sum(e_t)
+        col[8:16, rj] += folded_sum(e_s)
+    if j == i + 1:
+        row_t[ri] = e_t[:, :128] + e_t[:, 128:]
+        row_s[ri] = e_s[:, :128] + e_s[:, 128:]
+    elif j > i:
+        row_t[ri] += e_t[:, :128] + e_t[:, 128:]
+        row_s[ri] += e_s[:, :128] + e_s[:, 128:]
+
+
+def row_statistics(length, row_t, row_s, col, rvec, rb_t, rb_s, log_sum):
+    valid = lax.broadcasted_iota(jnp.int32, (1, N), 1) < length
+    padded = (N - length).astype(f32)
+
+    def total(row, c):
+        r = jnp.sum(row[0 : N - BL].T, axis=0, keepdims=True)
+        r = jnp.concatenate([r, jnp.zeros((1, BL), f32)], axis=1)
+        return jnp.where(valid, r + jnp.sum(c, axis=0, keepdims=True) - padded, 1.0)
+
+    sum_t, sum_s = total(row_t, col[0:8]), total(row_s, col[8:16])
+    r_t, r_s = jnp.where(valid, 1.0 / sum_t, 0.0), jnp.where(valid, 1.0 / sum_s, 0.0)
+    rvec[0:8] = jnp.broadcast_to(r_t, (8, N))
+    rvec[8:16] = jnp.broadcast_to(r_s, (8, N))
+    rb_t[...] = jnp.broadcast_to(r_t, (128, N)).T
+    rb_s[...] = jnp.broadcast_to(r_s, (128, N)).T
+    log_sum[0:1, :] += jnp.log2(sum_s) - jnp.log2(sum_t)
+
+
+def second_block(i, j, et, es, diff, rvec, rb_t, rb_s, both, kl):
+    ri, rj = pl.ds(i * BL, BL), pl.ds(j * BL, BL)
+
+    def pair(by_row, by_col):
+        wide = jnp.concatenate([by_row, by_row], axis=1).reshape(BL // 8, 8, BL)
+        return (wide + by_col[None]).reshape(BL, BL)
+
+    q_t = et[ri, rj] * pair(rb_t[ri], rvec[0:8, rj])
+    both[ri, rj] = (es[ri, rj] * pair(rb_s[ri], rvec[8:16, rj]) - q_t).astype(bf16)
+    part = folded_sum(q_t * diff[ri, rj])
+    kl[:, rj] += 0.5 * part if i == j else part
+
+
+def one_head(n, length, weight, ta, sb, bt, grad, lt, rt, ls, rs, et, es, diff, row_t, row_s, col, rvec, rb_t, rb_s, both, kl, log_sum):
+    h = Head(n)
+    right_operands(h, ta, sb, rt, rs)
+    for j in range(NB):
+        for i in range(j + 1):
+            first_block(i, j, h, lt, rt, ls, rs, et, es, diff, row_t, row_s, col)
+    row_statistics(length, row_t, row_s, col, rvec, rb_t, rb_s, log_sum)
+    for j in range(NB):
+        for i in range(j + 1):
+            second_block(i, j, et, es, diff, rvec, rb_t, rb_s, both, kl)
+    b = head_columns(h, bt)
+    scale = h.g_scale * weight
+    for j in range(NB):
+        lo, hi = j * BL, (j + 1) * BL
+        g = dot(b[:, :hi], both[0:hi, lo:hi], NN)
+        if hi < N:
+            g = g + dot(b[:, hi:], both[lo:hi, hi:N], NT)
+        grad[pl.ds(h.g_at, 32), lo:hi] += g * scale
+
+
+def bounded_kernel(
+    lengths, weights, tq, tk, tv, sq, sk, sv, loss, top, oq, ok, ov,
+    kv, rkv, rq, gq, gkv, rgkv, mine, theirs, t_sem, own_sem, send_sem, recv_sem, top_send, top_recv,
+    ta, sb, bt, grad, lt, rt, ls, rs, et, es, diff, row_t, row_s, col, rvec, rb_t, rb_s, both, kl, log_sum,
+):
+    owner, me = lax.axis_index("dp"), lax.axis_index("tensor")
+    length, weight = lengths[owner], weights[owner]
+    valid = lax.broadcasted_iota(jnp.int32, (N, 1), 0) < length
+    teacher = [
+        pltpu.make_async_copy(tq.at[0], ta.at[:, pl.ds(0, 1024)], t_sem.at[0]),
+        pltpu.make_async_copy(tk.at[0], ta.at[:, pl.ds(1024, 128)], t_sem.at[1]),
+        pltpu.make_async_copy(tv.at[0], ta.at[:, pl.ds(1152, 128)], t_sem.at[2]),
+    ]
+    for c in teacher:
+        c.start()
+    for t in range(TS):
+        kv[t] = fold_kv(sk[0, :, t * 32 : t * 32 + 32], sv[0, :, t * 32 : t * 32 + 32])
+
+    barrier = pltpu.get_barrier_semaphore()
+    for s in range(1, TS):
+        pl.semaphore_signal(
+            barrier, inc=1, device_id={"tensor": lax.rem(me + s, TS)}, device_id_type=MESH
+        )
+    def across(place, bit):
+        return place + bit - 2 * bit * lax.rem(place // bit, 2)
+
+    partners = [{"tensor": across(me, b)} for b in (1, 2, 4)]
+    partners += [{"dp": across(owner, b)} for b in (1, 2, 4, 8, 16)]
+    for p in partners[3:]:
+        pl.semaphore_signal(barrier, inc=1, device_id=p, device_id_type=MESH)
+    pl.semaphore_wait(barrier, TS - 1 + len(partners) - 3)
+
+    def bounds(k):
+        return pltpu.make_async_remote_copy(
+            src_ref=mine.at[k],
+            dst_ref=theirs.at[k],
+            send_sem=top_send.at[k],
+            recv_sem=top_recv.at[k],
+            device_id=partners[k],
+            device_id_type=MESH,
+        )
+
+    def at_rows(t):
+        return pl.ds(pl.multiple_of(t * ROWS, ROWS), ROWS)
+
+    def at_lanes(t, g=0, width=256):
+        return pl.ds(pl.multiple_of(t * 256 + g * 128, 128), width)
+
+    def ends(k, t):
+        return (
+            lambda: (kv.at[t], rkv.at[me]),
+            lambda: (sq.at[0, :, at_lanes(t)], rq.at[at_rows(me), :]),
+            lambda: (gq.at[0, at_rows(t), :], oq.at[0, :, at_lanes(me, 0, 128)]),
+            lambda: (gq.at[1, at_rows(t), :], oq.at[0, :, at_lanes(me, 1, 128)]),
+            lambda: (gkv.at[t], rgkv.at[me]),
+        )[k]()
+
+    def remote(k, s):
+        peer = lax.rem(me + s, TS)
+        src, dst = ends(k, peer)
+        return pltpu.make_async_remote_copy(
+            src_ref=src,
+            dst_ref=dst,
+            send_sem=send_sem.at[k, s],
+            recv_sem=recv_sem.at[k, s],
+            device_id={"tensor": peer},
+            device_id_type=MESH,
+        )
+
+    def own(k):
+        return pltpu.make_async_copy(*ends(k, me), own_sem.at[k])
+
+    def start(k):
+        for s in range(1, TS):
+            remote(k, s).start()
+        own(k).start()
+
+    def arrived(k):
+        own(k).wait()
+        for s in range(1, TS):
+            remote(k, s).wait_recv()
+
+    def sent(k):
+        for s in range(1, TS):
+            remote(k, s).wait_send()
+
+    start(0)
+    start(1)
+    grad[...] = jnp.zeros_like(grad)
+    kl[...] = jnp.zeros_like(kl)
+    log_sum[...] = jnp.zeros_like(log_sum)
+    for c in teacher:
+        c.wait()
+    set_teacher(valid, ta, lt)
+    arrived(0)
+    set_student_kv(valid, rkv, sb, bt, ls)
+
+    def leave(g):
+        x = grad[128 * g : 128 * g + 128].T
+        gq[g] = jnp.where(valid, x, 0.0).astype(bf16)
+        start(2 + g)
+
+    def step(n, carry):
+        @pl.when(n == HEADS)
+        def _():
+            arrived(1)
+            set_student_q(valid, rq, sb, bt, ls)
+            mine[0] = jnp.maximum(
+                jnp.maximum(bound_lanes(ta[:, 0:1024], 128), bound_lanes(ta[:, 1024:1280], 16)),
+                jnp.maximum(bound_lanes(sb[:, 0:256], 32), bound_lanes(sb[:, 256:512], 4)),
+            )
+            bounds(0).start()
+
+        for k in range(1, len(partners)):
+
+            @pl.when(n == HEADS + k)
+            def _():
+                bounds(k - 1).wait()
+                mine[k] = jnp.maximum(mine[k - 1], theirs[k - 1])
+                bounds(k).start()
+
+        @pl.when(n == HEADS + 4)
+        def _():
+            leave(0)
+
+        @pl.when(n == HEADS + 8)
+        def _():
+            leave(1)
+
+        one_head(n, length, weight, ta, sb, bt, grad, lt, rt, ls, rs, et, es, diff, row_t, row_s, col, rvec, rb_t, rb_s, both, kl, log_sum)
+        return carry
+
+    lax.fori_loop(0, 3 * HEADS, step, 0)
+    x = jnp.concatenate([grad[256:320], jnp.zeros((64, N), f32)], axis=0).T
+    x = jnp.where(valid, x, 0.0).astype(bf16).reshape(TS, 2, HALF, 128)
+    gkv[...] = jnp.concatenate([x[:, 0, :, 0:64], x[:, 1, :, 0:64]], axis=2)
+    start(4)
+    total = (jnp.sum(kl[...]) + jnp.sum(log_sum[...])) * math.log(2.0)
+    loss[0, 0] = total / length.astype(f32)
+    last = len(partners) - 1
+    bounds(last).wait()
+    top[0, 0] = jnp.max(jnp.maximum(mine[last], theirs[last]))
+    for k in range(2, 5):
+        arrived(k)
+    for i, out in enumerate((ok, ov)):
+        for half in range(2):
+            lo = half * 64 + i * 32
+            out[0, half * HALF : half * HALF + HALF, :] = jnp.concatenate(
+                [rgkv[t][:, lo : lo + 32] for t in range(TS)], axis=1
+            )
+    for k in range(5):
+        sent(k)
+
+
+def bounded_program(tq, tk, tv, sq, sk, sv, lengths, weights):
+    smem = pl.BlockSpec(memory_space=pltpu.SMEM)
+    vmem = pl.BlockSpec(memory_space=pltpu.VMEM)
+    hbm = pl.BlockSpec(memory_space=pl.ANY)
+    square = (N, N)
+    message = (TS, HALF, 128)
+    return pl.pallas_call(
+        bounded_kernel,
+        out_shape=(
+            jax.ShapeDtypeStruct((1, 1), f32),
+            jax.ShapeDtypeStruct((1, 1), f32),
+            jax.ShapeDtypeStruct((1, ROWS, 2048), bf16),
+            jax.ShapeDtypeStruct((1, ROWS, 256), bf16),
+            jax.ShapeDtypeStruct((1, ROWS, 256), bf16),
+        ),
+        in_specs=[smem, smem, hbm, hbm, hbm, hbm, vmem, vmem],
+        out_specs=[smem, smem, hbm, vmem, vmem],
+        scratch_shapes=[
+            pltpu.VMEM(message, bf16),
+            pltpu.VMEM(message, bf16),
+            pltpu.VMEM((N, 256), bf16),
+            pltpu.VMEM((2, N, 128), bf16),
+            pltpu.VMEM(message, bf16),
+            pltpu.VMEM(message, bf16),
+            pltpu.VMEM((8, 8, 128), f32),
+            pltpu.VMEM((8, 8, 128), f32),
+            pltpu.SemaphoreType.DMA((3,)),
+            pltpu.SemaphoreType.DMA((5,)),
+            pltpu.SemaphoreType.DMA((5, TS)),
+            pltpu.SemaphoreType.DMA((5, TS)),
+            pltpu.SemaphoreType.DMA((8,)),
+            pltpu.SemaphoreType.DMA((8,)),
+            pltpu.VMEM((N, 1280), bf16),
+            pltpu.VMEM((N, 512), bf16),
+            pltpu.VMEM((320, N), bf16),
+            pltpu.VMEM((320, N), f32),
+            pltpu.VMEM((N, 2560), bf16),
+            pltpu.VMEM((N, 128), bf16),
+            pltpu.VMEM((N, 1024), bf16),
+            pltpu.VMEM((N, 128), bf16),
+            pltpu.VMEM(square, f32),
+            pltpu.VMEM(square, f32),
+            pltpu.VMEM(square, f32),
+            pltpu.VMEM((N, 128), f32),
+            pltpu.VMEM((N, 128), f32),
+            pltpu.VMEM((16, N), f32),
+            pltpu.VMEM((16, N), f32),
+            pltpu.VMEM((N, 128), f32),
+            pltpu.VMEM((N, 128), f32),
+            pltpu.VMEM(square, bf16),
+            pltpu.VMEM((8, N), f32),
+            pltpu.VMEM((8, N), f32),
+        ],
+        compiler_params=pltpu.CompilerParams(
+            collective_id=0, has_side_effects=True, vmem_limit_bytes=VMEM_LIMIT
+        ),
+        cost_estimate=pl.CostEstimate(
+            flops=40 * 10**9, bytes_accessed=4 * 10**6, transcendentals=32 * 10**6
+        ),
+    )(lengths, weights, tq, tk, tv, sq, sk, sv)
+
+
+def keep_kernel(loss, q, k, v, loss_out, q_out, k_out, v_out):
+    loss_out[0, 0] = loss[0, 0]
+    q_out[...], k_out[...], v_out[...] = q[...], k[...], v[...]
+
+
+def keep(*results):
+    smem = pl.BlockSpec(memory_space=pltpu.SMEM)
+    specs = [smem] + [pl.BlockSpec(memory_space=pltpu.VMEM)] * 3
+    return pl.pallas_call(
+        keep_kernel,
+        out_shape=[jax.ShapeDtypeStruct(r.shape, r.dtype) for r in results],
+        in_specs=specs,
+        out_specs=specs,
+    )(*results)
+
+
+def on_device(*arrays):
+    loss, bound, *gradients = bounded_program(*arrays)
+    return lax.cond(
+        bound[0, 0] <= SAFE_LOG2,
+        lambda: tuple(keep(loss, *gradients)),
+        lambda: general_program(*arrays),
+    )
+
+
 def solution(mesh):
     in_specs = (
         P("dp", None, "tensor"),

time: 495 us -> 587 us (1.19); the launches traced: 492 us -> 577 us
  Pallas kernels: 0 us -> 83.1 us
    pallas_call x0 -> x1, Pallas kernels: none -> 83.1 us  [bounded_program(): pl.pallas_call(bounded_kernel, out_shape=(jax.ShapeDtypeStruct((1, 1), f3...]
    unnamed x29 -> x16, local copies, waits for them, and re-layouts: 16.4 us -> 0.03 us
    cond x0 -> x3, other arithmetic: none -> 8.37 us
    unnamed x3 -> x0, other arithmetic: 8.32 us -> none
    cond x0 -> x17, local copies, waits for them, and re-layouts: none -> 7.88 us
  transfers between devices with their start and end apart: 6 -> 6, of which waited for: 1 -> 1; matrix products, arithmetic and copies ran while one was open for 84% -> 72% of each run, Pallas kernels for 0% -> 0%
where the time goes in v2:
time: 587 us; the launch traced here: 577 us
  matrix products  221 us (38%)
  other arithmetic  161 us (27%)
  Pallas kernels  83.1 us (14%)
  local copies, waits for them, and re-layouts  37 us (6%)
  loops' own time  34.8 us (6%)
  starting transfers between devices  32.9 us (6%)
    dot_general x48, matrix products, head_terms(): jnp.dot(teach_rows, teach.T, preferred_element_type=jnp.float32)  117 us
    pallas_call x1, Pallas kernels, bounded_program(): pl.pallas_call(bounded_kernel, out_shape=(jax.ShapeDtypeStruct((1, 1), f3...  83.1 us
    dot_general x48, matrix products, head_terms(): jnp.dot(stud_rows, stud.T, preferred_element_type=jnp.float32) * stud_scale  66.3 us
    convert_element_type x24, other arithmetic, head_terms(): jnp.where(valid_rows[:, None], weight * (prob_stud - prob_teach), 0.0)  61.2 us
    another operation x3, loops' own time, kind_pass(): head_losses, gradients = lax.map(one_head, (teach_heads, stud_heads))  31.7 us
    lt x48, other arithmetic, head_terms(): valid_rows = row_start + jnp.arange(block_rows, dtype=jnp.int32) < length  30.6 us
    reduce_sum x24, other arithmetic, head_terms(): kl_total = kl_total + jnp.sum(jnp.where(valid_rows, row_divergence, 0.0))  30.3 us
    dot_general x48, matrix products, head_terms(): jnp.dot(slope_rows, stud, preferred_element_type=jnp.float32)  18.9 us
  transfers between devices with their start and end apart: 6, of which 1 were waited for; matrix products, arithmetic and copies ran while one was open for 72% of the time, Pallas kernels for 0%

profile of v2, /device:TPU:24, one launch (start us, length us, event | category | flops | bytes accessed | tf_op | source)
XLA Modules:
  0.0 576.6 jit_solution(11861514941833119861)
XLA Ops:
  0.7 83.1 %shard_map.119 = (f32[1,1]{1,0:T(1,128)}, f32[1,1]{1,0:T(1,128)}, bf16[1,128,2048]{2,1,0:T(8,128)(2,1)}, bf16[1,128,256]{2,1,0:T(8,128)(2,1)}, bf16[1,128,256]{2,1,0:T(8,128)(2,1)}) custom-call(s32[32]{0:T(128)} %lengths.1, f32[32]{0:T(128)} %weights.1, bf16[1,1024,1024]{2,1,0:T(8,128)(2,1)} %tq.1, bf16[1,1024,128]{2,1,0:T(8,128)(2,1)} %tk.1, ...), custom_call_target="tpu_custom_call" | custom-call | flops 40000000000 | bytes 4000000 | tf_op jit(solution)/shard_map/pallas_call | solution.py:459
  84.5 490.7 %conditional.1 = ((f32[1,1]{1,0:T(1,128)}, bf16[1,128,2048]{2,1,0:T(8,128)(2,1)}, bf16[1,128,256]{2,1,0:T(8,128)(2,1)}, bf16[1,128,256]{2,1,0:T(8,128)(2,1)})) conditional(s32[]{:T(128)} %bitcast.57, (bf16[1,1024,1024]{2,1,0:T(8,128)(2,1)S(1)}, bf16[1,128,2048]{2,1,0:T(8,128)(2,1)S(1)}, s32[32]{0:T(128)S(1)}, f32[32]{0:T(128)S(1)}, ...), branch_computations={%region_0.25_spmd, %region_24.26_spmd} | conditional | flops 681782272 | bytes 136926112 | solution.py:533
  85.3 4.3 all-to-all-start.1
  90.3 4.2 all-to-all-done.1
  94.5 4.7 all-to-all-start.2
  104.5 6.3 %all-to-all-start = ((bf16[1,128,8,256]{1,3,0,2:T(8,128)(2,1)}), bf16[1,128,8,256]{1,3,0,2:T(8,128)(2,1)S(1)}, u32[]{:S(2)}, u32[]{:S(2)}) async-start(bf16[1,128,8,256]{1,3,0,2:T(8,128)(2,1)} %bitcast.27), calls=%async_computation | async-start | bytes 1048576 | tf_op jit(solution)/shard_map/cond/branch_0_fun/all_to_all | solution.py:114
  110.8 118.5 %while.34 = (s32[]{:T(128)}, f32[8]{0:T(128)S(1)}, bf16[8,1024,4]{1,2,0:T(4,128)(2,1)S(1)}, s32[]{:T(128)}, bf16[8,1024,16]{1,2,0:T(8,128)(2,1)S(1)}, /*index=5*...) while((s32[]{:T(128)}, f32[8]{0:T(128)S(1)}, bf16[8,1024,4]{1,2,0:T(4,128)(2,1)S(1)}, ...), condition=%wide.region_15.16_spmd, body=%wide.region_10.15_spmd.sunk | while | flops 90199040 | bytes 33855164 | solution.py:76
  114.8 3.1 select_reduce_fusion.20
  129.6 3.1 select_reduce_fusion.20
  144.4 3.1 select_reduce_fusion.20
  159.2 3.1 select_reduce_fusion.20
  174.0 3.1 select_reduce_fusion.20
  188.8 3.1 select_reduce_fusion.20
  203.6 3.1 select_reduce_fusion.20
  218.4 3.1 select_reduce_fusion.20
  233.5 5.9 %all-to-all-start.4 = ((bf16[8,2,2048]{2,1,0:T(2,128)(2,1)}), bf16[8,2,2048]{2,1,0:T(2,128)(2,1)S(1)}, u32[]{:S(2)}, u32[]{:S(2)}) async-start(bf16[8,2,2048]{2,1,0:T(2,128)(2,1)} %reshape.119), calls=%async_computation.4 | async-start | bytes 131072 | tf_op jit(solution)/shard_map/cond/branch_0_fun/all_to_all | solution.py:125
  239.4 118.5 %while.35 = (s32[]{:T(128)}, f32[8]{0:T(128)S(1)}, bf16[8,1024,4]{1,2,0:T(4,128)(2,1)S(1)}, s32[]{:T(128)}, bf16[8,1024,16]{1,2,0:T(8,128)(2,1)S(1)}, /*index=5*...) while((s32[]{:T(128)}, f32[8]{0:T(128)S(1)}, bf16[8,1024,4]{1,2,0:T(4,128)(2,1)S(1)}, ...), condition=%wide.region_22.23_spmd, body=%wide.region_17.22_spmd.sunk | while | flops 90199040 | bytes 33855164 | solution.py:76
  243.4 3.1 select_reduce_fusion.22
  258.2 3.1 select_reduce_fusion.22
  273.0 3.1 select_reduce_fusion.22
  287.8 3.1 select_reduce_fusion.22
  302.6 3.1 select_reduce_fusion.22
  317.4 3.1 select_reduce_fusion.22
  332.2 3.1 select_reduce_fusion.22
  347.0 3.1 select_reduce_fusion.22
  362.1 6.0 %all-to-all-start.5 = ((bf16[8,2,2048]{2,1,0:T(2,128)(2,1)}), bf16[8,2,2048]{2,1,0:T(2,128)(2,1)}, u32[]{:S(2)}, u32[]{:S(2)}) async-start(bf16[8,2,2048]{2,1,0:T(2,128)(2,1)} %reshape.121), calls=%async_computation.5 | async-start | bytes 131072 | tf_op jit(solution)/shard_map/cond/branch_0_fun/all_to_all | solution.py:128
  368.1 184.0 %while.33 = (s32[]{:T(128)}, f32[8]{0:T(128)S(1)}, bf16[8,1024,32]{1,2,0:T(8,128)(2,1)}, s32[]{:T(128)}, bf16[8,1024,128]{1,2,0:T(8,128)(2,1)}, /*index=5*/bf16[8,1024,32]{1,2,0:T(8,128)(2,1)S(1)}, f32[]{:T(128)}, s32[]{:T(128)}) while((s32[]{:T(128)}, f32[8]{0:T(128)S(1)}, bf16[8,1024,32]{1,2,0:T(8,128)(2,1)}, s32[]{:T(128)}, ...), condition=%wide.region_8.9_spmd, body=%wide.region_1.8_spmd.sunk | while | flops 501384192 | bytes 45753008 | solution.py:76
  372.5 4.1 exponential_reduce_fusion.18
  377.4 4.8 select_reduce_fusion.18
  395.5 4.1 exponential_reduce_fusion.18
  400.4 4.8 select_reduce_fusion.18
  406.8 2.6 select_convert_fusion.9
  418.5 4.1 exponential_reduce_fusion.18
  423.4 4.8 select_reduce_fusion.18
  429.8 2.6 select_convert_fusion.9
  441.5 4.1 exponential_reduce_fusion.18
  446.4 4.8 select_reduce_fusion.18
  464.5 4.1 exponential_reduce_fusion.18
  469.4 4.8 select_reduce_fusion.18
  487.5 4.1 exponential_reduce_fusion.18
  492.4 4.8 select_reduce_fusion.18
  498.8 2.6 select_convert_fusion.9
  510.5 4.1 exponential_reduce_fusion.18
  515.4 4.8 select_reduce_fusion.18
  533.5 4.1 exponential_reduce_fusion.18
  538.4 4.8 select_reduce_fusion.18
  554.5 3.8 reduce
  559.3 5.7 all-to-all-start.3
  (574 shorter events, 285.8 us)
Async XLA Ops:
  0.6 83.8 %copy-start.1 = (bf16[1,1024,1024]{2,1,0:T(8,128)(2,1)S(1)}, bf16[1,1024,1024]{2,1,0:T(8,128)(2,1)}, u32[]{:S(2)}) copy-start(bf16[1,1024,1024]{2,1,0:T(8,128)(2,1)} %tq.1) | copy-start | bytes 6291460
  0.6 83.8 %copy-start.5 = (bf16[1,1024,128]{2,1,0:T(8,128)(2,1)S(1)}, bf16[1,1024,128]{2,1,0:T(8,128)(2,1)}, u32[]{:S(2)}) copy-start(bf16[1,1024,128]{2,1,0:T(8,128)(2,1)} %tk.1) | copy-start | bytes 786436
  0.7 83.8 %copy-start.6 = (bf16[1,1024,128]{2,1,0:T(8,128)(2,1)S(1)}, bf16[1,1024,128]{2,1,0:T(8,128)(2,1)}, u32[]{:S(2)}) copy-start(bf16[1,1024,128]{2,1,0:T(8,128)(2,1)} %tv.1) | copy-start | bytes 786436
  0.7 83.8 %copy-start.2 = (bf16[1,128,2048]{2,1,0:T(8,128)(2,1)S(1)}, bf16[1,128,2048]{2,1,0:T(8,128)(2,1)}, u32[]{:S(2)}) copy-start(bf16[1,128,2048]{2,1,0:T(8,128)(2,1)} %sq.1) | copy-start | bytes 1572868
  0.7 83.8 %copy-start.7 = (bf16[1,128,256]{2,1,0:T(8,128)(2,1)S(1)}, bf16[1,128,256]{2,1,0:T(8,128)(2,1)}, u32[]{:S(2)}) copy-start(bf16[1,128,256]{2,1,0:T(8,128)(2,1)} %sk.1) | copy-start | bytes 196612
  0.7 83.8 %copy-start.8 = (bf16[1,128,256]{2,1,0:T(8,128)(2,1)S(1)}, bf16[1,128,256]{2,1,0:T(8,128)(2,1)}, u32[]{:S(2)}) copy-start(bf16[1,128,256]{2,1,0:T(8,128)(2,1)} %sv.1) | copy-start | bytes 196612
  0.7 83.8 %copy-start.9 = (s32[32]{0:T(128)S(1)}, s32[32]{0:T(128)}, u32[]{:S(2)}) copy-start(s32[32]{0:T(128)} %lengths.1) | copy-start | bytes 388
  0.7 83.8 %copy-start.10 = (f32[32]{0:T(128)S(1)}, f32[32]{0:T(128)}, u32[]{:S(2)}) copy-start(f32[32]{0:T(128)} %weights.1) | copy-start | bytes 388
  85.3 9.2 %all-to-all-start.1 = ((bf16[1,128,8,32]{1,3,0,2:T(8,128)(2,1)}), bf16[1,128,8,32]{1,3,0,2:T(8,128)(2,1)S(1)}, u32[]{:S(2)}, u32[]{:S(2)}) async-start(bf16[1,128,8,32]{1,3,0,2:T(8,128)(2,1)} %bitcast.35), calls=%async_computation.1 | async-start | bytes 131072 | tf_op jit(solution)/shard_map/cond/branch_0_fun/all_to_all | solution.py:115
  94.5 10.0 %all-to-all-start.2 = ((bf16[1,128,8,32]{1,3,0,2:T(8,128)(2,1)}), bf16[1,128,8,32]{1,3,0,2:T(8,128)(2,1)S(1)}, u32[]{:S(2)}, u32[]{:S(2)}) async-start(bf16[1,128,8,32]{1,3,0,2:T(8,128)(2,1)} %bitcast.42), calls=%async_computation.2 | async-start | bytes 131072 | tf_op jit(solution)/shard_map/cond/branch_0_fun/all_to_all | solution.py:116
  104.5 129.0 %all-to-all-start = ((bf16[1,128,8,256]{1,3,0,2:T(8,128)(2,1)}), bf16[1,128,8,256]{1,3,0,2:T(8,128)(2,1)S(1)}, u32[]{:S(2)}, u32[]{:S(2)}) async-start(bf16[1,128,8,256]{1,3,0,2:T(8,128)(2,1)} %bitcast.27), calls=%async_computation | async-start | bytes 1048576 | tf_op jit(solution)/shard_map/cond/branch_0_fun/all_to_all | solution.py:114
  233.5 128.6 %all-to-all-start.4 = ((bf16[8,2,2048]{2,1,0:T(2,128)(2,1)}), bf16[8,2,2048]{2,1,0:T(2,128)(2,1)S(1)}, u32[]{:S(2)}, u32[]{:S(2)}) async-start(bf16[8,2,2048]{2,1,0:T(2,128)(2,1)} %reshape.119), calls=%async_computation.4 | async-start | bytes 131072 | tf_op jit(solution)/shard_map/cond/branch_0_fun/all_to_all | solution.py:125
  362.1 6.0 %copy-start.3 = (bf16[8,2,2048]{2,1,0:T(2,128)(2,1)}, bf16[8,2,2048]{2,1,0:T(2,128)(2,1)S(1)}, u32[]{:S(2)}) copy-start(bf16[8,2,2048]{2,1,0:T(2,128)(2,1)S(1)} %all-to-all-done.4) | copy-start | bytes 196612 | tf_op jit(solution)/shard_map/cond
  362.1 197.2 %all-to-all-start.5 = ((bf16[8,2,2048]{2,1,0:T(2,128)(2,1)}), bf16[8,2,2048]{2,1,0:T(2,128)(2,1)}, u32[]{:S(2)}, u32[]{:S(2)}) async-start(bf16[8,2,2048]{2,1,0:T(2,128)(2,1)} %reshape.121), calls=%async_computation.5 | async-start | bytes 131072 | tf_op jit(solution)/shard_map/cond/branch_0_fun/all_to_all | solution.py:128
  382.2 1.6 copy-start
  405.2 1.6 copy-start
  428.2 1.6 copy-start
  451.2 1.6 copy-start
  474.2 1.6 copy-start
  497.2 1.6 copy-start
  520.2 1.6 copy-start
  543.2 1.6 copy-start
  554.5 12.4 %copy-start.4 = (bf16[8,2,2048]{2,1,0:T(2,128)(2,1)S(1)}, bf16[8,2,2048]{2,1,0:T(2,128)(2,1)}, u32[]{:S(2)}) copy-start(bf16[8,2,2048]{2,1,0:T(2,128)(2,1)} %copy-done.3) | copy-start | bytes 196612 | tf_op jit(solution)/shard_map/cond
  559.3 13.8 %all-to-all-start.3 = ((bf16[8,2,16384]{2,1,0:T(2,128)(2,1)}), bf16[8,2,16384]{2,1,0:T(2,128)(2,1)S(1)}, u32[]{:S(2)}, u32[]{:S(2)}) async-start(bf16[8,2,16384]{2,1,0:T(2,128)(2,1)} %reshape.117), calls=%async_computation.3 | async-start | bytes 1048576 | tf_op jit(solution)/shard_map/cond/branch_0_fun/all_to_all | solution.py:122

commit v3 on v2

--- a/solution.py
+++ b/solution.py
@@ -153,8 +153,10 @@
         q = (n >= HEADS) & (n < 2 * HEADS)
         kv = jnp.where(n < HEADS, 0, 1)
         sub = lax.rem(n, HEADS)
-        self.t_at = pl.multiple_of(jnp.where(q, sub, HEADS + kv) * 128, 128)
-        self.s_at = pl.multiple_of(jnp.where(q, sub // 4, 2 + kv) * 128, 128)
+        self.t_group = jnp.where(q, sub, HEADS + kv)
+        self.s_group = jnp.where(q, sub // 4, 2 + kv)
+        self.t_at = pl.multiple_of(self.t_group * 128, 128)
+        self.s_at = pl.multiple_of(self.s_group * 128, 128)
         self.g_at = pl.multiple_of(jnp.where(q, 32 * sub, 256 + 32 * kv), 32)
         self.t_scale = jnp.where(q, LOG2E * 128**-0.5, LOG2E * 0.25).astype(f32)
         self.s_scale = jnp.where(q, LOG2E * 32**-0.5, LOG2E * 0.5).astype(f32)
@@ -170,8 +172,8 @@
 def split_scaled(x, scale, left, at):
     y = x.astype(f32) * scale
     top = y.astype(bf16)
-    left[:, at : at + 128] = top
-    left[:, at + 128 : at + 256] = (y - top.astype(f32)).astype(bf16)
+    left[at, :, 0:128] = top
+    left[at, :, 128:256] = (y - top.astype(f32)).astype(bf16)
 
 
 def set_teacher(valid, ta, lt):
@@ -179,7 +181,7 @@
         at = g * 128
         x = jnp.where(valid, ta[:, at : at + 128].astype(f32), 0.0).astype(bf16)
         ta[:, at : at + 128] = x
-        split_scaled(x, LOG2E * (128**-0.5 if g < HEADS else 0.25), lt, 2 * at)
+        split_scaled(x, LOG2E * (128**-0.5 if g < HEADS else 0.25), lt, g)
 
 
 def set_student_kv(valid, rkv, sb, bt, ls):
@@ -191,7 +193,7 @@
         at = 256 + 128 * i
         sb[:, at : at + 128] = b.astype(bf16)
         bt[256 + 32 * i : 288 + 32 * i] = b.T[0:32].astype(bf16)
-        split_scaled(b.astype(bf16), LOG2E * 0.5, ls, 2 * at)
+        split_scaled(b.astype(bf16), LOG2E * 0.5, ls, 2 + i)
 
 
 def set_student_q(valid, rq, sb, bt, ls):
@@ -200,7 +202,7 @@
         b = jnp.where(valid, rq[:, at : at + 128].astype(f32), 0.0)
         sb[:, at : at + 128] = b.astype(bf16)
         bt[at : at + 128] = b.T.astype(bf16)
-        split_scaled(b.astype(bf16), LOG2E * 32**-0.5, ls, 2 * at)
+        split_scaled(b.astype(bf16), LOG2E * 32**-0.5, ls, g)
 
 
 def right_operands(h, ta, sb, rt, rs):
@@ -225,8 +227,8 @@
 
 def first_block(i, j, h, lt, rt, ls, rs, et, es, diff, row_t, row_s, col):
     ri, rj = pl.ds(i * BL, BL), pl.ds(j * BL, BL)
-    x_t = dot(lt[ri, pl.ds(2 * h.t_at, 256)], jnp.concatenate([rt[rj], rt[rj]], axis=1), NT)
-    x_s = dot(ls[ri, pl.ds(2 * h.s_at, 256)], jnp.concatenate([rs[rj], rs[rj]], axis=1), NT)
+    x_t = dot(lt[h.t_group, ri], jnp.concatenate([rt[rj], rt[rj]], axis=1), NT)
+    x_s = dot(ls[h.s_group, ri], jnp.concatenate([rs[rj], rs[rj]], axis=1), NT)
     e_t, e_s = jnp.exp2(x_t), jnp.exp2(x_s)
     et[ri, rj] = e_t
     es[ri, rj] = e_s
@@ -276,16 +278,8 @@
     kl[:, rj] += 0.5 * part if i == j else part
 
 
-def one_head(n, length, weight, ta, sb, bt, grad, lt, rt, ls, rs, et, es, diff, row_t, row_s, col, rvec, rb_t, rb_s, both, kl, log_sum):
+def gradient(n, weight, bt, grad, both):
     h = Head(n)
-    right_operands(h, ta, sb, rt, rs)
-    for j in range(NB):
-        for i in range(j + 1):
-            first_block(i, j, h, lt, rt, ls, rs, et, es, diff, row_t, row_s, col)
-    row_statistics(length, row_t, row_s, col, rvec, rb_t, rb_s, log_sum)
-    for j in range(NB):
-        for i in range(j + 1):
-            second_block(i, j, et, es, diff, rvec, rb_t, rb_s, both, kl)
     b = head_columns(h, bt)
     scale = h.g_scale * weight
     for j in range(NB):
@@ -296,9 +290,22 @@
         grad[pl.ds(h.g_at, 32), lo:hi] += g * scale
 
 
+def one_head(n, length, weight, ta, sb, bt, grad, lt, rt, ls, rs, et, es, diff, row_t, row_s, col, rvec, rb_t, rb_s, both, kl, log_sum):
+    h = Head(n)
+    right_operands(h, ta, sb, rt, rs)
+    for j in range(NB):
+        for i in range(j + 1):
+            first_block(i, j, h, lt, rt, ls, rs, et, es, diff, row_t, row_s, col)
+    row_statistics(length, row_t, row_s, col, rvec, rb_t, rb_s, log_sum)
+    gradient(jnp.maximum(n - 1, 0), weight, bt, grad, both)
+    for j in range(NB):
+        for i in range(j + 1):
+            second_block(i, j, et, es, diff, rvec, rb_t, rb_s, both, kl)
+
+
 def bounded_kernel(
     lengths, weights, tq, tk, tv, sq, sk, sv, loss, top, oq, ok, ov,
-    kv, rkv, rq, gq, gkv, rgkv, mine, theirs, t_sem, own_sem, send_sem, recv_sem, top_send, top_recv,
+    kv, rkv, rq, gq, gkv, rgkv, mine, theirs, t_sem, own_sem, send_sem, recv_sem,
     ta, sb, bt, grad, lt, rt, ls, rs, et, es, diff, row_t, row_s, col, rvec, rb_t, rb_s, both, kl, log_sum,
 ):
     owner, me = lax.axis_index("dp"), lax.axis_index("tensor")
@@ -319,24 +326,7 @@
         pl.semaphore_signal(
             barrier, inc=1, device_id={"tensor": lax.rem(me + s, TS)}, device_id_type=MESH
         )
-    def across(place, bit):
-        return place + bit - 2 * bit * lax.rem(place // bit, 2)
-
-    partners = [{"tensor": across(me, b)} for b in (1, 2, 4)]
-    partners += [{"dp": across(owner, b)} for b in (1, 2, 4, 8, 16)]
-    for p in partners[3:]:
-        pl.semaphore_signal(barrier, inc=1, device_id=p, device_id_type=MESH)
-    pl.semaphore_wait(barrier, TS - 1 + len(partners) - 3)
-
-    def bounds(k):
-        return pltpu.make_async_remote_copy(
-            src_ref=mine.at[k],
-            dst_ref=theirs.at[k],
-            send_sem=top_send.at[k],
-            recv_sem=top_recv.at[k],
-            device_id=partners[k],
-            device_id_type=MESH,
-        )
+    pl.semaphore_wait(barrier, TS - 1)
 
     def at_rows(t):
         return pl.ds(pl.multiple_of(t * ROWS, ROWS), ROWS)
@@ -351,6 +341,7 @@
             lambda: (gq.at[0, at_rows(t), :], oq.at[0, :, at_lanes(me, 0, 128)]),
             lambda: (gq.at[1, at_rows(t), :], oq.at[0, :, at_lanes(me, 1, 128)]),
             lambda: (gkv.at[t], rgkv.at[me]),
+            lambda: (mine, theirs.at[me]),
         )[k]()
 
     def remote(k, s):
@@ -383,14 +374,15 @@
             remote(k, s).wait_send()
 
     start(0)
-    start(1)
     grad[...] = jnp.zeros_like(grad)
     kl[...] = jnp.zeros_like(kl)
     log_sum[...] = jnp.zeros_like(log_sum)
+    both[...] = jnp.zeros_like(both)
     for c in teacher:
         c.wait()
     set_teacher(valid, ta, lt)
     arrived(0)
+    start(1)
     set_student_kv(valid, rkv, sb, bt, ls)
 
     def leave(g):
@@ -403,25 +395,17 @@
         def _():
             arrived(1)
             set_student_q(valid, rq, sb, bt, ls)
-            mine[0] = jnp.maximum(
+            mine[...] = jnp.maximum(
                 jnp.maximum(bound_lanes(ta[:, 0:1024], 128), bound_lanes(ta[:, 1024:1280], 16)),
                 jnp.maximum(bound_lanes(sb[:, 0:256], 32), bound_lanes(sb[:, 256:512], 4)),
             )
-            bounds(0).start()
-
-        for k in range(1, len(partners)):
-
-            @pl.when(n == HEADS + k)
-            def _():
-                bounds(k - 1).wait()
-                mine[k] = jnp.maximum(mine[k - 1], theirs[k - 1])
-                bounds(k).start()
-
-        @pl.when(n == HEADS + 4)
+            start(5)
+
+        @pl.when(n == HEADS + 5)
         def _():
             leave(0)
 
-        @pl.when(n == HEADS + 8)
+        @pl.when(n == HEADS + 9)
         def _():
             leave(1)
 
@@ -429,15 +413,15 @@
         return carry
 
     lax.fori_loop(0, 3 * HEADS, step, 0)
+    gradient(3 * HEADS - 1, weight, bt, grad, both)
     x = jnp.concatenate([grad[256:320], jnp.zeros((64, N), f32)], axis=0).T
     x = jnp.where(valid, x, 0.0).astype(bf16).reshape(TS, 2, HALF, 128)
     gkv[...] = jnp.concatenate([x[:, 0, :, 0:64], x[:, 1, :, 0:64]], axis=2)
     start(4)
     total = (jnp.sum(kl[...]) + jnp.sum(log_sum[...])) * math.log(2.0)
     loss[0, 0] = total / length.astype(f32)
-    last = len(partners) - 1
-    bounds(last).wait()
-    top[0, 0] = jnp.max(jnp.maximum(mine[last], theirs[last]))
+    arrived(5)
+    top[0, 0] = jnp.max(theirs[...])
     for k in range(2, 5):
         arrived(k)
     for i, out in enumerate((ok, ov)):
@@ -446,7 +430,7 @@
             out[0, half * HALF : half * HALF + HALF, :] = jnp.concatenate(
                 [rgkv[t][:, lo : lo + 32] for t in range(TS)], axis=1
             )
-    for k in range(5):
+    for k in range(6):
         sent(k)
 
 
@@ -474,21 +458,19 @@
             pltpu.VMEM((2, N, 128), bf16),
             pltpu.VMEM(message, bf16),
             pltpu.VMEM(message, bf16),
-            pltpu.VMEM((8, 8, 128), f32),
-            pltpu.VMEM((8, 8, 128), f32),
+            pltpu.VMEM((8, 128), f32),
+            pltpu.VMEM((TS, 8, 128), f32),
             pltpu.SemaphoreType.DMA((3,)),
-            pltpu.SemaphoreType.DMA((5,)),
-            pltpu.SemaphoreType.DMA((5, TS)),
-            pltpu.SemaphoreType.DMA((5, TS)),
-            pltpu.SemaphoreType.DMA((8,)),
-            pltpu.SemaphoreType.DMA((8,)),
+            pltpu.SemaphoreType.DMA((6,)),
+            pltpu.SemaphoreType.DMA((6, TS)),
+            pltpu.SemaphoreType.DMA((6, TS)),
             pltpu.VMEM((N, 1280), bf16),
             pltpu.VMEM((N, 512), bf16),
             pltpu.VMEM((320, N), bf16),
             pltpu.VMEM((320, N), f32),
-            pltpu.VMEM((N, 2560), bf16),
+            pltpu.VMEM((HEADS + 2, N, 256), bf16),
             pltpu.VMEM((N, 128), bf16),
-            pltpu.VMEM((N, 1024), bf16),
+            pltpu.VMEM((4, N, 256), bf16),
             pltpu.VMEM((N, 128), bf16),
             pltpu.VMEM(square, f32),
             pltpu.VMEM(square, f32),

time: 587 us -> 571 us (0.973)
  Pallas kernels: 83.1 us -> 66.9 us
    pallas_call x1, Pallas kernels: 83.1 us -> 66.9 us  [bounded_program(): pl.pallas_call(bounded_kernel, out_shape=(jax.ShapeDtypeStruct((1, 1), f3...]
  transfers between devices with their start and end apart: 6 -> 6, of which waited for: 1 -> 1; matrix products, arithmetic and copies ran while one was open for 72% -> 74% of each run, Pallas kernels for 0% -> 0%
where the time goes in v3:
time: 571 us; the launch traced here: 561 us
  matrix products  221 us (39%)
  other arithmetic  161 us (28%)
  Pallas kernels  66.9 us (12%)
  local copies, waits for them, and re-layouts  37 us (6%)
  loops' own time  34.9 us (6%)
  starting transfers between devices  32.8 us (6%)
    dot_general x48, matrix products, head_terms(): jnp.dot(teach_rows, teach.T, preferred_element_type=jnp.float32)  117 us
    pallas_call x1, Pallas kernels, bounded_program(): pl.pallas_call(bounded_kernel, out_shape=(jax.ShapeDtypeStruct((1, 1), f3...  66.9 us
    dot_general x48, matrix products, head_terms(): jnp.dot(stud_rows, stud.T, preferred_element_type=jnp.float32) * stud_scale  66.3 us
    convert_element_type x24, other arithmetic, head_terms(): jnp.where(valid_rows[:, None], weight * (prob_stud - prob_teach), 0.0)  61.2 us
    another operation x3, loops' own time, kind_pass(): head_losses, gradients = lax.map(one_head, (teach_heads, stud_heads))  31.7 us
    lt x48, other arithmetic, head_terms(): valid_rows = row_start + jnp.arange(block_rows, dtype=jnp.int32) < length  30.6 us
    reduce_sum x24, other arithmetic, head_terms(): kl_total = kl_total + jnp.sum(jnp.where(valid_rows, row_divergence, 0.0))  30.3 us
    dot_general x48, matrix products, head_terms(): jnp.dot(slope_rows, stud, preferred_element_type=jnp.float32)  18.9 us
  transfers between devices with their start and end apart: 6, of which 1 were waited for; matrix products, arithmetic and copies ran while one was open for 74% of the time, Pallas kernels for 0%

profile of v3, /device:TPU:24, one launch (start us, length us, event | category | flops | bytes accessed | tf_op | source)
XLA Modules:
  0.0 560.5 jit_solution(10303284100578278068)
XLA Ops:
  0.7 66.9 %shard_map.119 = (f32[1,1]{1,0:T(1,128)}, f32[1,1]{1,0:T(1,128)}, bf16[1,128,2048]{2,1,0:T(8,128)(2,1)}, bf16[1,128,256]{2,1,0:T(8,128)(2,1)}, bf16[1,128,256]{2,1,0:T(8,128)(2,1)}) custom-call(s32[32]{0:T(128)} %lengths.1, f32[32]{0:T(128)} %weights.1, bf16[1,1024,1024]{2,1,0:T(8,128)(2,1)} %tq.1, bf16[1,1024,128]{2,1,0:T(8,128)(2,1)} %tk.1, ...), custom_call_target="tpu_custom_call" | custom-call | flops 40000000000 | bytes 4000000 | tf_op jit(solution)/shard_map/pallas_call | solution.py:443
  68.3 490.6 %conditional.1 = ((f32[1,1]{1,0:T(1,128)}, bf16[1,128,2048]{2,1,0:T(8,128)(2,1)}, bf16[1,128,256]{2,1,0:T(8,128)(2,1)}, bf16[1,128,256]{2,1,0:T(8,128)(2,1)})) conditional(s32[]{:T(128)} %bitcast.57, (bf16[1,1024,1024]{2,1,0:T(8,128)(2,1)S(1)}, bf16[1,128,2048]{2,1,0:T(8,128)(2,1)S(1)}, s32[32]{0:T(128)S(1)}, f32[32]{0:T(128)S(1)}, ...), branch_computations={%region_0.25_spmd, %region_24.26_spmd} | conditional | flops 681782272 | bytes 136926112 | solution.py:515
  69.1 4.4 all-to-all-start.1
  74.2 4.1 all-to-all-done.1
  78.3 4.8 all-to-all-start.2
  88.3 5.9 %all-to-all-start = ((bf16[1,128,8,256]{1,3,0,2:T(8,128)(2,1)}), bf16[1,128,8,256]{1,3,0,2:T(8,128)(2,1)S(1)}, u32[]{:S(2)}, u32[]{:S(2)}) async-start(bf16[1,128,8,256]{1,3,0,2:T(8,128)(2,1)} %bitcast.27), calls=%async_computation | async-start | bytes 1048576 | tf_op jit(solution)/shard_map/cond/branch_0_fun/all_to_all | solution.py:114
  94.3 118.5 %while.34 = (s32[]{:T(128)}, f32[8]{0:T(128)S(1)}, bf16[8,1024,4]{1,2,0:T(4,128)(2,1)S(1)}, s32[]{:T(128)}, bf16[8,1024,16]{1,2,0:T(8,128)(2,1)S(1)}, /*index=5*...) while((s32[]{:T(128)}, f32[8]{0:T(128)S(1)}, bf16[8,1024,4]{1,2,0:T(4,128)(2,1)S(1)}, ...), condition=%wide.region_15.16_spmd, body=%wide.region_10.15_spmd.sunk | while | flops 90199040 | bytes 33855164 | solution.py:76
  98.3 3.1 select_reduce_fusion.20
  113.1 3.1 select_reduce_fusion.20
  127.9 3.1 select_reduce_fusion.20
  142.7 3.1 select_reduce_fusion.20
  157.5 3.1 select_reduce_fusion.20
  172.3 3.1 select_reduce_fusion.20
  187.1 3.1 select_reduce_fusion.20
  201.9 3.1 select_reduce_fusion.20
  217.0 5.9 %all-to-all-start.4 = ((bf16[8,2,2048]{2,1,0:T(2,128)(2,1)}), bf16[8,2,2048]{2,1,0:T(2,128)(2,1)S(1)}, u32[]{:S(2)}, u32[]{:S(2)}) async-start(bf16[8,2,2048]{2,1,0:T(2,128)(2,1)} %reshape.119), calls=%async_computation.4 | async-start | bytes 131072 | tf_op jit(solution)/shard_map/cond/branch_0_fun/all_to_all | solution.py:125
  223.0 118.4 %while.35 = (s32[]{:T(128)}, f32[8]{0:T(128)S(1)}, bf16[8,1024,4]{1,2,0:T(4,128)(2,1)S(1)}, s32[]{:T(128)}, bf16[8,1024,16]{1,2,0:T(8,128)(2,1)S(1)}, /*index=5*...) while((s32[]{:T(128)}, f32[8]{0:T(128)S(1)}, bf16[8,1024,4]{1,2,0:T(4,128)(2,1)S(1)}, ...), condition=%wide.region_22.23_spmd, body=%wide.region_17.22_spmd.sunk | while | flops 90199040 | bytes 33855164 | solution.py:76
  227.0 3.1 select_reduce_fusion.22
  241.8 3.1 select_reduce_fusion.22
  256.6 3.1 select_reduce_fusion.22
  271.4 3.1 select_reduce_fusion.22
  286.2 3.1 select_reduce_fusion.22
  301.0 3.1 select_reduce_fusion.22
  315.8 3.1 select_reduce_fusion.22
  330.6 3.1 select_reduce_fusion.22
  345.6 6.0 %all-to-all-start.5 = ((bf16[8,2,2048]{2,1,0:T(2,128)(2,1)}), bf16[8,2,2048]{2,1,0:T(2,128)(2,1)}, u32[]{:S(2)}, u32[]{:S(2)}) async-start(bf16[8,2,2048]{2,1,0:T(2,128)(2,1)} %reshape.121), calls=%async_computation.5 | async-start | bytes 131072 | tf_op jit(solution)/shard_map/cond/branch_0_fun/all_to_all | solution.py:128
  351.7 184.0 %while.33 = (s32[]{:T(128)}, f32[8]{0:T(128)S(1)}, bf16[8,1024,32]{1,2,0:T(8,128)(2,1)}, s32[]{:T(128)}, bf16[8,1024,128]{1,2,0:T(8,128)(2,1)}, /*index=5*/bf16[8,1024,32]{1,2,0:T(8,128)(2,1)S(1)}, f32[]{:T(128)}, s32[]{:T(128)}) while((s32[]{:T(128)}, f32[8]{0:T(128)S(1)}, bf16[8,1024,32]{1,2,0:T(8,128)(2,1)}, s32[]{:T(128)}, ...), condition=%wide.region_8.9_spmd, body=%wide.region_1.8_spmd.sunk | while | flops 501384192 | bytes 45753008 | solution.py:76
  356.1 4.1 exponential_reduce_fusion.18
  361.0 4.8 select_reduce_fusion.18
  367.4 2.6 select_convert_fusion.9
  379.1 4.1 exponential_reduce_fusion.18
  384.0 4.8 select_reduce_fusion.18
  402.1 4.1 exponential_reduce_fusion.18
  407.0 4.8 select_reduce_fusion.18
  425.1 4.1 exponential_reduce_fusion.18
  430.0 4.8 select_reduce_fusion.18
  436.4 2.6 select_convert_fusion.9
  448.1 4.1 exponential_reduce_fusion.18
  453.0 4.8 select_reduce_fusion.18
  459.4 2.6 select_convert_fusion.9
  471.1 4.1 exponential_reduce_fusion.18
  476.0 4.8 select_reduce_fusion.18
  494.1 4.1 exponential_reduce_fusion.18
  499.0 4.8 select_reduce_fusion.18
  517.1 4.1 exponential_reduce_fusion.18
  522.0 4.8 select_reduce_fusion.18
  538.1 3.8 reduce
  542.9 5.7 %all-to-all-start.3 = ((bf16[8,2,16384]{2,1,0:T(2,128)(2,1)}), bf16[8,2,16384]{2,1,0:T(2,128)(2,1)S(1)}, u32[]{:S(2)}, u32[]{:S(2)}) async-start(bf16[8,2,16384]{2,1,0:T(2,128)(2,1)} %reshape.117), calls=%async_computation.3 | async-start | bytes 1048576 | tf_op jit(solution)/shard_map/cond/branch_0_fun/all_to_all | solution.py:122
  (574 shorter events, 285.8 us)
Async XLA Ops:
  0.6 67.6 %copy-start.1 = (bf16[1,1024,1024]{2,1,0:T(8,128)(2,1)S(1)}, bf16[1,1024,1024]{2,1,0:T(8,128)(2,1)}, u32[]{:S(2)}) copy-start(bf16[1,1024,1024]{2,1,0:T(8,128)(2,1)} %tq.1) | copy-start | bytes 6291460
  0.6 67.6 %copy-start.5 = (bf16[1,1024,128]{2,1,0:T(8,128)(2,1)S(1)}, bf16[1,1024,128]{2,1,0:T(8,128)(2,1)}, u32[]{:S(2)}) copy-start(bf16[1,1024,128]{2,1,0:T(8,128)(2,1)} %tk.1) | copy-start | bytes 786436
  0.7 67.6 %copy-start.6 = (bf16[1,1024,128]{2,1,0:T(8,128)(2,1)S(1)}, bf16[1,1024,128]{2,1,0:T(8,128)(2,1)}, u32[]{:S(2)}) copy-start(bf16[1,1024,128]{2,1,0:T(8,128)(2,1)} %tv.1) | copy-start | bytes 786436
  0.7 67.6 %copy-start.2 = (bf16[1,128,2048]{2,1,0:T(8,128)(2,1)S(1)}, bf16[1,128,2048]{2,1,0:T(8,128)(2,1)}, u32[]{:S(2)}) copy-start(bf16[1,128,2048]{2,1,0:T(8,128)(2,1)} %sq.1) | copy-start | bytes 1572868
  0.7 67.6 %copy-start.7 = (bf16[1,128,256]{2,1,0:T(8,128)(2,1)S(1)}, bf16[1,128,256]{2,1,0:T(8,128)(2,1)}, u32[]{:S(2)}) copy-start(bf16[1,128,256]{2,1,0:T(8,128)(2,1)} %sk.1) | copy-start | bytes 196612
  0.7 67.6 %copy-start.8 = (bf16[1,128,256]{2,1,0:T(8,128)(2,1)S(1)}, bf16[1,128,256]{2,1,0:T(8,128)(2,1)}, u32[]{:S(2)}) copy-start(bf16[1,128,256]{2,1,0:T(8,128)(2,1)} %sv.1) | copy-start | bytes 196612
  0.7 67.6 %copy-start.9 = (s32[32]{0:T(128)S(1)}, s32[32]{0:T(128)}, u32[]{:S(2)}) copy-start(s32[32]{0:T(128)} %lengths.1) | copy-start | bytes 388
  0.7 67.6 %copy-start.10 = (f32[32]{0:T(128)S(1)}, f32[32]{0:T(128)}, u32[]{:S(2)}) copy-start(f32[32]{0:T(128)} %weights.1) | copy-start | bytes 388
  69.1 9.3 %all-to-all-start.1 = ((bf16[1,128,8,32]{1,3,0,2:T(8,128)(2,1)}), bf16[1,128,8,32]{1,3,0,2:T(8,128)(2,1)S(1)}, u32[]{:S(2)}, u32[]{:S(2)}) async-start(bf16[1,128,8,32]{1,3,0,2:T(8,128)(2,1)} %bitcast.35), calls=%async_computation.1 | async-start | bytes 131072 | tf_op jit(solution)/shard_map/cond/branch_0_fun/all_to_all | solution.py:115
  78.3 10.0 %all-to-all-start.2 = ((bf16[1,128,8,32]{1,3,0,2:T(8,128)(2,1)}), bf16[1,128,8,32]{1,3,0,2:T(8,128)(2,1)S(1)}, u32[]{:S(2)}, u32[]{:S(2)}) async-start(bf16[1,128,8,32]{1,3,0,2:T(8,128)(2,1)} %bitcast.42), calls=%async_computation.2 | async-start | bytes 131072 | tf_op jit(solution)/shard_map/cond/branch_0_fun/all_to_all | solution.py:116
  88.3 128.7 %all-to-all-start = ((bf16[1,128,8,256]{1,3,0,2:T(8,128)(2,1)}), bf16[1,128,8,256]{1,3,0,2:T(8,128)(2,1)S(1)}, u32[]{:S(2)}, u32[]{:S(2)}) async-start(bf16[1,128,8,256]{1,3,0,2:T(8,128)(2,1)} %bitcast.27), calls=%async_computation | async-start | bytes 1048576 | tf_op jit(solution)/shard_map/cond/branch_0_fun/all_to_all | solution.py:114
  217.0 128.6 %all-to-all-start.4 = ((bf16[8,2,2048]{2,1,0:T(2,128)(2,1)}), bf16[8,2,2048]{2,1,0:T(2,128)(2,1)S(1)}, u32[]{:S(2)}, u32[]{:S(2)}) async-start(bf16[8,2,2048]{2,1,0:T(2,128)(2,1)} %reshape.119), calls=%async_computation.4 | async-start | bytes 131072 | tf_op jit(solution)/shard_map/cond/branch_0_fun/all_to_all | solution.py:125
  345.6 6.1 %copy-start.3 = (bf16[8,2,2048]{2,1,0:T(2,128)(2,1)}, bf16[8,2,2048]{2,1,0:T(2,128)(2,1)S(1)}, u32[]{:S(2)}) copy-start(bf16[8,2,2048]{2,1,0:T(2,128)(2,1)S(1)} %all-to-all-done.4) | copy-start | bytes 196612 | tf_op jit(solution)/shard_map/cond
  345.6 197.3 %all-to-all-start.5 = ((bf16[8,2,2048]{2,1,0:T(2,128)(2,1)}), bf16[8,2,2048]{2,1,0:T(2,128)(2,1)}, u32[]{:S(2)}, u32[]{:S(2)}) async-start(bf16[8,2,2048]{2,1,0:T(2,128)(2,1)} %reshape.121), calls=%async_computation.5 | async-start | bytes 131072 | tf_op jit(solution)/shard_map/cond/branch_0_fun/all_to_all | solution.py:128
  365.8 1.6 copy-start
  388.8 1.6 copy-start
  411.8 1.6 copy-start
  434.8 1.6 copy-start
  457.8 1.6 copy-start
  480.8 1.6 copy-start
  503.8 1.6 copy-start
  526.8 1.6 copy-start
  538.1 12.4 %copy-start.4 = (bf16[8,2,2048]{2,1,0:T(2,128)(2,1)S(1)}, bf16[8,2,2048]{2,1,0:T(2,128)(2,1)}, u32[]{:S(2)}) copy-start(bf16[8,2,2048]{2,1,0:T(2,128)(2,1)} %copy-done.3) | copy-start | bytes 196612 | tf_op jit(solution)/shard_map/cond
  542.9 13.8 %all-to-all-start.3 = ((bf16[8,2,16384]{2,1,0:T(2,128)(2,1)}), bf16[8,2,16384]{2,1,0:T(2,128)(2,1)S(1)}, u32[]{:S(2)}, u32[]{:S(2)}) async-start(bf16[8,2,16384]{2,1,0:T(2,128)(2,1)} %reshape.117), calls=%async_computation.3 | async-start | bytes 1048576 | tf_op jit(solution)/shard_map/cond/branch_0_fun/all_to_all | solution.py:122

commit v4 on v3

--- a/solution.py
+++ b/solution.py
@@ -310,6 +310,11 @@
 ):
     owner, me = lax.axis_index("dp"), lax.axis_index("tensor")
     length, weight = lengths[owner], weights[owner]
+    barrier = pltpu.get_barrier_semaphore()
+    for s in range(1, TS):
+        pl.semaphore_signal(
+            barrier, inc=1, device_id={"tensor": lax.rem(me + s, TS)}, device_id_type=MESH
+        )
     valid = lax.broadcasted_iota(jnp.int32, (N, 1), 0) < length
     teacher = [
         pltpu.make_async_copy(tq.at[0], ta.at[:, pl.ds(0, 1024)], t_sem.at[0]),
@@ -321,11 +326,6 @@
     for t in range(TS):
         kv[t] = fold_kv(sk[0, :, t * 32 : t * 32 + 32], sv[0, :, t * 32 : t * 32 + 32])
 
-    barrier = pltpu.get_barrier_semaphore()
-    for s in range(1, TS):
-        pl.semaphore_signal(
-            barrier, inc=1, device_id={"tensor": lax.rem(me + s, TS)}, device_id_type=MESH
-        )
     pl.semaphore_wait(barrier, TS - 1)
 
     def at_rows(t):
@@ -340,8 +340,9 @@
             lambda: (sq.at[0, :, at_lanes(t)], rq.at[at_rows(me), :]),
             lambda: (gq.at[0, at_rows(t), :], oq.at[0, :, at_lanes(me, 0, 128)]),
             lambda: (gq.at[1, at_rows(t), :], oq.at[0, :, at_lanes(me, 1, 128)]),
-            lambda: (gkv.at[t], rgkv.at[me]),
+            lambda: (gkv.at[0, t], rgkv.at[0, me]),
             lambda: (mine, theirs.at[me]),
+            lambda: (gkv.at[1, t], rgkv.at[1, me]),
         )[k]()
 
     def remote(k, s):
@@ -390,6 +391,21 @@
         gq[g] = jnp.where(valid, x, 0.0).astype(bf16)
         start(2 + g)
 
+    quarter = ROWS // 4
+
+    def leave_kv(i):
+        x = jnp.concatenate([grad[256 + 32 * i : 288 + 32 * i], jnp.zeros((96, N), f32)], axis=0).T
+        x = jnp.where(valid, x, 0.0).astype(bf16).reshape(TS, 4, quarter, 128)
+        gkv[i] = jnp.concatenate([x[:, r, :, 0:32] for r in range(4)], axis=2)
+        start(4 + 2 * i)
+
+    def take_kv(i, out):
+        arrived(4 + 2 * i)
+        for r in range(4):
+            out[0, r * quarter : (r + 1) * quarter, :] = jnp.concatenate(
+                [rgkv[i, t][:, 32 * r : 32 * r + 32] for t in range(TS)], axis=1
+            )
+
     def step(n, carry):
         @pl.when(n == HEADS)
         def _():
@@ -401,6 +417,14 @@
             )
             start(5)
 
+        @pl.when(n == HEADS + 1)
+        def _():
+            leave_kv(0)
+
+        @pl.when(n == 2 * HEADS)
+        def _():
+            take_kv(0, ok)
+
         @pl.when(n == HEADS + 5)
         def _():
             leave(0)
@@ -414,23 +438,15 @@
 
     lax.fori_loop(0, 3 * HEADS, step, 0)
     gradient(3 * HEADS - 1, weight, bt, grad, both)
-    x = jnp.concatenate([grad[256:320], jnp.zeros((64, N), f32)], axis=0).T
-    x = jnp.where(valid, x, 0.0).astype(bf16).reshape(TS, 2, HALF, 128)
-    gkv[...] = jnp.concatenate([x[:, 0, :, 0:64], x[:, 1, :, 0:64]], axis=2)
-    start(4)
+    leave_kv(1)
     total = (jnp.sum(kl[...]) + jnp.sum(log_sum[...])) * math.log(2.0)
     loss[0, 0] = total / length.astype(f32)
     arrived(5)
     top[0, 0] = jnp.max(theirs[...])
-    for k in range(2, 5):
-        arrived(k)
-    for i, out in enumerate((ok, ov)):
-        for half in range(2):
-            lo = half * 64 + i * 32
-            out[0, half * HALF : half * HALF + HALF, :] = jnp.concatenate(
-                [rgkv[t][:, lo : lo + 32] for t in range(TS)], axis=1
-            )
-    for k in range(6):
+    arrived(2)
+    arrived(3)
+    take_kv(1, ov)
+    for k in range(7):
         sent(k)
 
 
@@ -456,14 +472,14 @@
             pltpu.VMEM(message, bf16),
             pltpu.VMEM((N, 256), bf16),
             pltpu.VMEM((2, N, 128), bf16),
-            pltpu.VMEM(message, bf16),
-            pltpu.VMEM(message, bf16),
+            pltpu.VMEM((2, TS, ROWS // 4, 128), bf16),
+            pltpu.VMEM((2, TS, ROWS // 4, 128), bf16),
             pltpu.VMEM((8, 128), f32),
             pltpu.VMEM((TS, 8, 128), f32),
             pltpu.SemaphoreType.DMA((3,)),
-            pltpu.SemaphoreType.DMA((6,)),
-            pltpu.SemaphoreType.DMA((6, TS)),
-            pltpu.SemaphoreType.DMA((6, TS)),
+            pltpu.SemaphoreType.DMA((7,)),
+            pltpu.SemaphoreType.DMA((7, TS)),
+            pltpu.SemaphoreType.DMA((7, TS)),
             pltpu.VMEM((N, 1280), bf16),
             pltpu.VMEM((N, 512), bf16),
             pltpu.VMEM((320, N), bf16),
@@ -494,19 +510,24 @@
     )(lengths, weights, tq, tk, tv, sq, sk, sv)
 
 
-def keep_kernel(loss, q, k, v, loss_out, q_out, k_out, v_out):
+def keep_kernel(loss, q, k, v, loss_out, q_out, k_out, v_out, sem):
+    pairs = ((q, q_out), (k, k_out), (v, v_out))
+    copies = [pltpu.make_async_copy(a, b, sem.at[i]) for i, (a, b) in enumerate(pairs)]
+    for c in copies:
+        c.start()
     loss_out[0, 0] = loss[0, 0]
-    q_out[...], k_out[...], v_out[...] = q[...], k[...], v[...]
+    for c in copies:
+        c.wait()
 
 
 def keep(*results):
-    smem = pl.BlockSpec(memory_space=pltpu.SMEM)
-    specs = [smem] + [pl.BlockSpec(memory_space=pltpu.VMEM)] * 3
+    specs = [pl.BlockSpec(memory_space=pltpu.SMEM)] + [pl.BlockSpec(memory_space=pl.ANY)] * 3
     return pl.pallas_call(
         keep_kernel,
         out_shape=[jax.ShapeDtypeStruct(r.shape, r.dtype) for r in results],
         in_specs=specs,
         out_specs=specs,
+        scratch_shapes=[pltpu.SemaphoreType.DMA((3,))],
     )(*results)
 
 

time: 571 us -> 572 us (level)
  no operation moved by 1% of the time
where the time goes in v4:
time: 572 us; the launch traced here: 561 us
  matrix products  221 us (39%)
  other arithmetic  161 us (28%)
  Pallas kernels  67.4 us (12%)
  local copies, waits for them, and re-layouts  37 us (6%)
  loops' own time  34.9 us (6%)
  starting transfers between devices  32.9 us (6%)
    dot_general x48, matrix products, head_terms(): jnp.dot(teach_rows, teach.T, preferred_element_type=jnp.float32)  117 us
    pallas_call x1, Pallas kernels, bounded_program(): pl.pallas_call(bounded_kernel, out_shape=(jax.ShapeDtypeStruct((1, 1), f3...  67.4 us
    dot_general x48, matrix products, head_terms(): jnp.dot(stud_rows, stud.T, preferred_element_type=jnp.float32) * stud_scale  66.3 us
    convert_element_type x24, other arithmetic, head_terms(): jnp.where(valid_rows[:, None], weight * (prob_stud - prob_teach), 0.0)  61.2 us
    another operation x3, loops' own time, kind_pass(): head_losses, gradients = lax.map(one_head, (teach_heads, stud_heads))  31.7 us
    lt x48, other arithmetic, head_terms(): valid_rows = row_start + jnp.arange(block_rows, dtype=jnp.int32) < length  30.6 us
    reduce_sum x24, other arithmetic, head_terms(): kl_total = kl_total + jnp.sum(jnp.where(valid_rows, row_divergence, 0.0))  30.3 us
    dot_general x48, matrix products, head_terms(): jnp.dot(slope_rows, stud, preferred_element_type=jnp.float32)  18.9 us
  transfers between devices with their start and end apart: 6, of which 1 were waited for; matrix products, arithmetic and copies ran while one was open for 74% of the time, Pallas kernels for 0%

profile of v4, /device:TPU:24, one launch (start us, length us, event | category | flops | bytes accessed | tf_op | source)
XLA Modules:
  0.0 561.2 jit_solution(12220046688414471911)
XLA Ops:
  0.7 67.4 %shard_map.119 = (f32[1,1]{1,0:T(1,128)}, f32[1,1]{1,0:T(1,128)}, bf16[1,128,2048]{2,1,0:T(8,128)(2,1)}, bf16[1,128,256]{2,1,0:T(8,128)(2,1)}, bf16[1,128,256]{2,1,0:T(8,128)(2,1)}) custom-call(s32[32]{0:T(128)} %lengths.1, f32[32]{0:T(128)} %weights.1, bf16[1,1024,1024]{2,1,0:T(8,128)(2,1)} %tq.1, bf16[1,1024,128]{2,1,0:T(8,128)(2,1)} %tk.1, ...), custom_call_target="tpu_custom_call" | custom-call | flops 40000000000 | bytes 4000000 | tf_op jit(solution)/shard_map/pallas_call | solution.py:459
  68.9 490.7 %conditional.1 = ((f32[1,1]{1,0:T(1,128)}, bf16[1,128,2048]{2,1,0:T(8,128)(2,1)}, bf16[1,128,256]{2,1,0:T(8,128)(2,1)}, bf16[1,128,256]{2,1,0:T(8,128)(2,1)})) conditional(s32[]{:T(128)} %bitcast.57, (bf16[1,1024,1024]{2,1,0:T(8,128)(2,1)S(1)}, bf16[1,128,2048]{2,1,0:T(8,128)(2,1)S(1)}, s32[32]{0:T(128)S(1)}, f32[32]{0:T(128)S(1)}, ...), branch_computations={%region_0.25_spmd, %region_24.26_spmd} | conditional | flops 681782272 | bytes 136926112 | solution.py:536
  69.6 4.6 all-to-all-start.1
  74.9 4.1 all-to-all-done.1
  79.0 4.8 all-to-all-start.2
  89.0 5.9 %all-to-all-start = ((bf16[1,128,8,256]{1,3,0,2:T(8,128)(2,1)}), bf16[1,128,8,256]{1,3,0,2:T(8,128)(2,1)S(1)}, u32[]{:S(2)}, u32[]{:S(2)}) async-start(bf16[1,128,8,256]{1,3,0,2:T(8,128)(2,1)} %bitcast.27), calls=%async_computation | async-start | bytes 1048576 | tf_op jit(solution)/shard_map/cond/branch_0_fun/all_to_all | solution.py:114
  95.0 118.5 %while.34 = (s32[]{:T(128)}, f32[8]{0:T(128)S(1)}, bf16[8,1024,4]{1,2,0:T(4,128)(2,1)S(1)}, s32[]{:T(128)}, bf16[8,1024,16]{1,2,0:T(8,128)(2,1)S(1)}, /*index=5*...) while((s32[]{:T(128)}, f32[8]{0:T(128)S(1)}, bf16[8,1024,4]{1,2,0:T(4,128)(2,1)S(1)}, ...), condition=%wide.region_15.16_spmd, body=%wide.region_10.15_spmd.sunk | while | flops 90199040 | bytes 33855164 | solution.py:76
  99.0 3.1 select_reduce_fusion.20
  113.8 3.1 select_reduce_fusion.20
  128.6 3.1 select_reduce_fusion.20
  143.4 3.1 select_reduce_fusion.20
  158.2 3.1 select_reduce_fusion.20
  173.1 3.1 select_reduce_fusion.20
  187.9 3.1 select_reduce_fusion.20
  202.7 3.1 select_reduce_fusion.20
  217.7 5.9 %all-to-all-start.4 = ((bf16[8,2,2048]{2,1,0:T(2,128)(2,1)}), bf16[8,2,2048]{2,1,0:T(2,128)(2,1)S(1)}, u32[]{:S(2)}, u32[]{:S(2)}) async-start(bf16[8,2,2048]{2,1,0:T(2,128)(2,1)} %reshape.119), calls=%async_computation.4 | async-start | bytes 131072 | tf_op jit(solution)/shard_map/cond/branch_0_fun/all_to_all | solution.py:125
  223.7 118.4 %while.35 = (s32[]{:T(128)}, f32[8]{0:T(128)S(1)}, bf16[8,1024,4]{1,2,0:T(4,128)(2,1)S(1)}, s32[]{:T(128)}, bf16[8,1024,16]{1,2,0:T(8,128)(2,1)S(1)}, /*index=5*...) while((s32[]{:T(128)}, f32[8]{0:T(128)S(1)}, bf16[8,1024,4]{1,2,0:T(4,128)(2,1)S(1)}, ...), condition=%wide.region_22.23_spmd, body=%wide.region_17.22_spmd.sunk | while | flops 90199040 | bytes 33855164 | solution.py:76
  227.7 3.1 select_reduce_fusion.22
  242.5 3.1 select_reduce_fusion.22
  257.3 3.1 select_reduce_fusion.22
  272.1 3.1 select_reduce_fusion.22
  286.9 3.1 select_reduce_fusion.22
  301.7 3.1 select_reduce_fusion.22
  316.5 3.1 select_reduce_fusion.22
  331.3 3.1 select_reduce_fusion.22
  346.4 6.0 %all-to-all-start.5 = ((bf16[8,2,2048]{2,1,0:T(2,128)(2,1)}), bf16[8,2,2048]{2,1,0:T(2,128)(2,1)}, u32[]{:S(2)}, u32[]{:S(2)}) async-start(bf16[8,2,2048]{2,1,0:T(2,128)(2,1)} %reshape.121), calls=%async_computation.5 | async-start | bytes 131072 | tf_op jit(solution)/shard_map/cond/branch_0_fun/all_to_all | solution.py:128
  352.4 184.0 %while.33 = (s32[]{:T(128)}, f32[8]{0:T(128)S(1)}, bf16[8,1024,32]{1,2,0:T(8,128)(2,1)}, s32[]{:T(128)}, bf16[8,1024,128]{1,2,0:T(8,128)(2,1)}, /*index=5*/bf16[8,1024,32]{1,2,0:T(8,128)(2,1)S(1)}, f32[]{:T(128)}, s32[]{:T(128)}) while((s32[]{:T(128)}, f32[8]{0:T(128)S(1)}, bf16[8,1024,32]{1,2,0:T(8,128)(2,1)}, s32[]{:T(128)}, ...), condition=%wide.region_8.9_spmd, body=%wide.region_1.8_spmd.sunk | while | flops 501384192 | bytes 45753008 | solution.py:76
  356.8 4.1 exponential_reduce_fusion.18
  361.7 4.8 select_reduce_fusion.18
  368.1 2.6 select_convert_fusion.9
  379.8 4.1 exponential_reduce_fusion.18
  384.7 4.8 select_reduce_fusion.18
  391.1 2.6 select_convert_fusion.9
  402.8 4.1 exponential_reduce_fusion.18
  407.7 4.8 select_reduce_fusion.18
  425.8 4.1 exponential_reduce_fusion.18
  430.7 4.8 select_reduce_fusion.18
  437.1 2.6 select_convert_fusion.9
  448.8 4.1 exponential_reduce_fusion.18
  453.7 4.8 select_reduce_fusion.18
  471.8 4.1 exponential_reduce_fusion.18
  476.7 4.8 select_reduce_fusion.18
  494.8 4.1 exponential_reduce_fusion.18
  499.7 4.8 select_reduce_fusion.18
  517.8 4.1 exponential_reduce_fusion.18
  522.7 4.8 select_reduce_fusion.18
  538.8 3.8 reduce
  543.6 5.7 %all-to-all-start.3 = ((bf16[8,2,16384]{2,1,0:T(2,128)(2,1)}), bf16[8,2,16384]{2,1,0:T(2,128)(2,1)S(1)}, u32[]{:S(2)}, u32[]{:S(2)}) async-start(bf16[8,2,16384]{2,1,0:T(2,128)(2,1)} %reshape.117), calls=%async_computation.3 | async-start | bytes 1048576 | tf_op jit(solution)/shard_map/cond/branch_0_fun/all_to_all | solution.py:122
  (574 shorter events, 285.8 us)
Async XLA Ops:
  0.6 68.2 %copy-start.1 = (bf16[1,1024,1024]{2,1,0:T(8,128)(2,1)S(1)}, bf16[1,1024,1024]{2,1,0:T(8,128)(2,1)}, u32[]{:S(2)}) copy-start(bf16[1,1024,1024]{2,1,0:T(8,128)(2,1)} %tq.1) | copy-start | bytes 6291460
  0.6 68.2 %copy-start.5 = (bf16[1,1024,128]{2,1,0:T(8,128)(2,1)S(1)}, bf16[1,1024,128]{2,1,0:T(8,128)(2,1)}, u32[]{:S(2)}) copy-start(bf16[1,1024,128]{2,1,0:T(8,128)(2,1)} %tk.1) | copy-start | bytes 786436
  0.7 68.2 %copy-start.6 = (bf16[1,1024,128]{2,1,0:T(8,128)(2,1)S(1)}, bf16[1,1024,128]{2,1,0:T(8,128)(2,1)}, u32[]{:S(2)}) copy-start(bf16[1,1024,128]{2,1,0:T(8,128)(2,1)} %tv.1) | copy-start | bytes 786436
  0.7 68.2 %copy-start.2 = (bf16[1,128,2048]{2,1,0:T(8,128)(2,1)S(1)}, bf16[1,128,2048]{2,1,0:T(8,128)(2,1)}, u32[]{:S(2)}) copy-start(bf16[1,128,2048]{2,1,0:T(8,128)(2,1)} %sq.1) | copy-start | bytes 1572868
  0.7 68.2 %copy-start.7 = (bf16[1,128,256]{2,1,0:T(8,128)(2,1)S(1)}, bf16[1,128,256]{2,1,0:T(8,128)(2,1)}, u32[]{:S(2)}) copy-start(bf16[1,128,256]{2,1,0:T(8,128)(2,1)} %sk.1) | copy-start | bytes 196612
  0.7 68.2 %copy-start.8 = (bf16[1,128,256]{2,1,0:T(8,128)(2,1)S(1)}, bf16[1,128,256]{2,1,0:T(8,128)(2,1)}, u32[]{:S(2)}) copy-start(bf16[1,128,256]{2,1,0:T(8,128)(2,1)} %sv.1) | copy-start | bytes 196612
  0.7 68.2 %copy-start.9 = (s32[32]{0:T(128)S(1)}, s32[32]{0:T(128)}, u32[]{:S(2)}) copy-start(s32[32]{0:T(128)} %lengths.1) | copy-start | bytes 388
  0.7 68.2 %copy-start.10 = (f32[32]{0:T(128)S(1)}, f32[32]{0:T(128)}, u32[]{:S(2)}) copy-start(f32[32]{0:T(128)} %weights.1) | copy-start | bytes 388
  69.6 9.4 %all-to-all-start.1 = ((bf16[1,128,8,32]{1,3,0,2:T(8,128)(2,1)}), bf16[1,128,8,32]{1,3,0,2:T(8,128)(2,1)S(1)}, u32[]{:S(2)}, u32[]{:S(2)}) async-start(bf16[1,128,8,32]{1,3,0,2:T(8,128)(2,1)} %bitcast.35), calls=%async_computation.1 | async-start | bytes 131072 | tf_op jit(solution)/shard_map/cond/branch_0_fun/all_to_all | solution.py:115
  79.0 10.0 %all-to-all-start.2 = ((bf16[1,128,8,32]{1,3,0,2:T(8,128)(2,1)}), bf16[1,128,8,32]{1,3,0,2:T(8,128)(2,1)S(1)}, u32[]{:S(2)}, u32[]{:S(2)}) async-start(bf16[1,128,8,32]{1,3,0,2:T(8,128)(2,1)} %bitcast.42), calls=%async_computation.2 | async-start | bytes 131072 | tf_op jit(solution)/shard_map/cond/branch_0_fun/all_to_all | solution.py:116
  89.0 128.7 %all-to-all-start = ((bf16[1,128,8,256]{1,3,0,2:T(8,128)(2,1)}), bf16[1,128,8,256]{1,3,0,2:T(8,128)(2,1)S(1)}, u32[]{:S(2)}, u32[]{:S(2)}) async-start(bf16[1,128,8,256]{1,3,0,2:T(8,128)(2,1)} %bitcast.27), calls=%async_computation | async-start | bytes 1048576 | tf_op jit(solution)/shard_map/cond/branch_0_fun/all_to_all | solution.py:114
  217.7 128.6 %all-to-all-start.4 = ((bf16[8,2,2048]{2,1,0:T(2,128)(2,1)}), bf16[8,2,2048]{2,1,0:T(2,128)(2,1)S(1)}, u32[]{:S(2)}, u32[]{:S(2)}) async-start(bf16[8,2,2048]{2,1,0:T(2,128)(2,1)} %reshape.119), calls=%async_computation.4 | async-start | bytes 131072 | tf_op jit(solution)/shard_map/cond/branch_0_fun/all_to_all | solution.py:125
  346.3 6.1 %copy-start.3 = (bf16[8,2,2048]{2,1,0:T(2,128)(2,1)}, bf16[8,2,2048]{2,1,0:T(2,128)(2,1)S(1)}, u32[]{:S(2)}) copy-start(bf16[8,2,2048]{2,1,0:T(2,128)(2,1)S(1)} %all-to-all-done.4) | copy-start | bytes 196612 | tf_op jit(solution)/shard_map/cond
  346.4 197.3 %all-to-all-start.5 = ((bf16[8,2,2048]{2,1,0:T(2,128)(2,1)}), bf16[8,2,2048]{2,1,0:T(2,128)(2,1)}, u32[]{:S(2)}, u32[]{:S(2)}) async-start(bf16[8,2,2048]{2,1,0:T(2,128)(2,1)} %reshape.121), calls=%async_computation.5 | async-start | bytes 131072 | tf_op jit(solution)/shard_map/cond/branch_0_fun/all_to_all | solution.py:128
  366.5 1.6 copy-start
  389.5 1.6 copy-start
  412.5 1.6 copy-start
  435.5 1.6 copy-start
  458.5 1.6 copy-start
  481.5 1.6 copy-start
  504.5 1.6 copy-start
  527.5 1.6 copy-start
  538.8 12.4 %copy-start.4 = (bf16[8,2,2048]{2,1,0:T(2,128)(2,1)S(1)}, bf16[8,2,2048]{2,1,0:T(2,128)(2,1)}, u32[]{:S(2)}) copy-start(bf16[8,2,2048]{2,1,0:T(2,128)(2,1)} %copy-done.3) | copy-start | bytes 196612 | tf_op jit(solution)/shard_map/cond
  543.6 13.8 %all-to-all-start.3 = ((bf16[8,2,16384]{2,1,0:T(2,128)(2,1)}), bf16[8,2,16384]{2,1,0:T(2,128)(2,1)S(1)}, u32[]{:S(2)}, u32[]{:S(2)}) async-start(bf16[8,2,16384]{2,1,0:T(2,128)(2,1)} %reshape.117), calls=%async_computation.3 | async-start | bytes 1048576 | tf_op jit(solution)/shard_map/cond/branch_0_fun/all_to_all | solution.py:122
